TPU v7x, 256 devices: a whole 4x4x8 slice. The times are simulated.
256 devices in a mesh: side: 2 (over core), seq: 16 (over x, y), tensor: 8 (over z).
Axes of the slice: x: 4, y: 4, z: 8, core: 2. Of those that a mesh axis runs over, the one named last changes fastest.
Arguments:
- x_rows: bfloat16 [512, 8192], P(('side', 'seq')), may hold values from -40 to 40
- attn_gain: bfloat16 [8192], replicated, may hold values from 0.25 to 1.75
- final_gain: bfloat16 [8192], replicated, may hold values from 0.25 to 1.75
- w_query: bfloat16 [8192, 8192], P(('side', 'seq'), 'tensor'), may hold values from -0.0625 to 0.0625
- w_kv: bfloat16 [8192, 2, 1024], P(('side', 'seq'), None, 'tensor'), may hold values from -0.15625 to 0.15625
- w_out: bfloat16 [8192, 8192], P('tensor', ('side', 'seq')), may hold values from -0.0625 to 0.0625
- kv_cache: bfloat16 [2, 4, 32768, 1024], P(None, None, ('side', 'seq'), 'tensor'), may hold values from -1500 to 1500
- w_vocab: bfloat16 [8192, 152064], P(None, ('side', 'seq', 'tensor')), may hold values from -16 to 16
- token_ids: int32 [512], replicated, may hold values from 0 to 152063
- cache_len: int32 [4], replicated, may hold values from 8192 to 32768, as said below
- row_traj: int32 [512], replicated, may hold values from 0 to 3, as said below
Outputs:
- attended: bfloat16 [512, 8192], P('tensor', ('side', 'seq'))
- logprob: float32 [512], replicated
Inputs may be any that keep to these rules, and one draw needn't show every extreme that they name: `row_traj`: each of the 4 trajectories owns exactly 128 rows. `cache_len`: at least one trajectory's cache is full.
All inputs are finite; a program needn't handle non-finite values.
Results may differ from a plain program's by a relative error of at most 0.02.
Values may be sent and summed in bfloat16 or wider, within the bound.
A program may use at most 192 MiB of HBM per device.

v0:
```python
import math

import jax
import jax.numpy as jnp
from jax import lax
from jax.sharding import PartitionSpec as P

HD = 128
TRAJ = 4


epsilon = 1e-06
rope_base = 1000000.0
masked_low = -1e30


def rms_scale(rows_in, gain_vec):
    values = rows_in.astype(jnp.float32)
    mean_sq = jnp.mean(values * values, axis=-1, keepdims=True)
    return (values * lax.rsqrt(mean_sq + epsilon) * gain_vec.astype(jnp.float32)).astype(
        jnp.bfloat16
    )


def row_places(row_traj, cache_len, traj_count):
    member = (row_traj[:, None] == jnp.arange(traj_count, dtype=jnp.int32)[None, :]).astype(
        jnp.int32
    )
    running = jnp.cumsum(member, axis=0)
    step_index = jnp.sum(running * member, axis=1) - 1
    places = jnp.sum(member * cache_len[None, :], axis=1) + step_index
    return (step_index, places)


def rope_angles(places, head_dim):
    half_dim = head_dim // 2
    spread = jnp.exp(
        jnp.arange(half_dim).astype(jnp.float32) * (-2.0 * math.log(rope_base) / head_dim)
    )
    return places.astype(jnp.float32)[:, None, None] * spread[None, None, :]


def rotate_half(values, angles):
    half_dim = values.shape[-1] // 2
    cosine = jnp.cos(angles)
    sine_part = jnp.sin(angles)
    leading = values[..., :half_dim]
    trailing = values[..., half_dim:]
    return jnp.concatenate(
        [leading * cosine - trailing * sine_part, trailing * cosine + leading * sine_part], axis=-1
    )


def block_terms(queries, keys_block, values_block, allowed, scale):
    scores = (
        jnp.einsum("bskgd,bpkd->bskgp", queries, keys_block, preferred_element_type=jnp.float32)
        * scale
    )
    peak_score = jnp.max(jnp.where(allowed, scores, masked_low), axis=-1)
    weights = jnp.where(allowed, jnp.exp(scores - peak_score[..., None]), 0.0)
    weight_sum = jnp.sum(weights, axis=-1)
    block_out = jnp.einsum(
        "bskgp,bpkd->bskgd",
        weights.astype(jnp.bfloat16),
        values_block,
        preferred_element_type=jnp.float32,
    )
    return (peak_score, weight_sum, block_out)


def combine(earlier, later):
    joined = jnp.maximum(earlier[0], later[0])
    first_scale = jnp.exp(earlier[0] - joined)
    second_scale = jnp.exp(later[0] - joined)
    return (
        joined,
        earlier[1] * first_scale + later[1] * second_scale,
        earlier[2] * first_scale[..., None] + later[2] * second_scale[..., None],
    )


def per_device(
    x_rows,
    attn_gain,
    final_gain,
    w_query,
    w_kv,
    w_out,
    kv_cache,
    w_vocab,
    token_ids,
    cache_len,
    row_traj,
):
    normed = rms_scale(x_rows, attn_gain)
    raw_block, norm_block = (
        lax.all_to_all(x_rows, ("side", "seq"), split_axis=1, concat_axis=0, tiled=True),
        lax.all_to_all(normed, ("side", "seq"), split_axis=1, concat_axis=0, tiled=True),
    )
    row_count = raw_block.shape[0]
    feature_block = raw_block.shape[1]
    query_part = jnp.dot(norm_block, w_query, preferred_element_type=jnp.float32)
    pair_part = jnp.dot(
        norm_block, w_kv.reshape(feature_block, -1), preferred_element_type=jnp.float32
    )
    heads_here = query_part.shape[1] // HD
    kv_here = pair_part.shape[1] // (2 * HD)
    group_size = heads_here // kv_here
    per_traj = row_count // TRAJ
    step_index, places = row_places(row_traj, cache_len, TRAJ)
    angles = rope_angles(places, HD)
    query_sum, pair_sum = lax.psum((query_part, pair_part), ("side", "seq"))
    queries = rotate_half(query_sum.reshape(row_count, heads_here, HD), angles).astype(jnp.bfloat16)
    pair_rows = pair_sum.reshape(row_count, 2, kv_here, HD)
    new_keys = rotate_half(pair_rows[:, 0], angles).astype(jnp.bfloat16)
    new_values = pair_rows[:, 1].astype(jnp.bfloat16)
    slots = row_traj * per_traj + step_index
    placing = (jnp.arange(row_count, dtype=jnp.int32)[:, None] == slots[None, :]).astype(
        jnp.bfloat16
    )
    sorted_q = jnp.dot(
        placing, queries.reshape(row_count, -1), preferred_element_type=jnp.float32
    ).astype(jnp.bfloat16)
    sorted_q = sorted_q.reshape(TRAJ, per_traj, kv_here, group_size, HD)
    fresh_rows = jnp.concatenate(
        [new_keys.reshape(row_count, -1), new_values.reshape(row_count, -1)], axis=1
    )
    sorted_new = jnp.dot(placing, fresh_rows, preferred_element_type=jnp.float32).astype(
        jnp.bfloat16
    )
    sorted_new = sorted_new.reshape(TRAJ, per_traj, 2, kv_here, HD)
    cache_dev = kv_cache.shape[2]
    cache_keys = kv_cache[0].reshape(TRAJ, cache_dev, kv_here, HD)
    cache_values = kv_cache[1].reshape(TRAJ, cache_dev, kv_here, HD)
    first_place = lax.axis_index(("side", "seq")) * cache_dev
    positions = first_place + jnp.arange(cache_dev, dtype=jnp.int32)
    allowed = (positions[None, :] < cache_len[:, None])[:, None, None, None, :]
    scale = float(HD) ** (-0.5)
    partial_value = block_terms(sorted_q, cache_keys, cache_values, allowed, scale)
    causal = (jnp.arange(per_traj)[None, :] <= jnp.arange(per_traj)[:, None])[
        None, :, None, None, :
    ]
    own_part = block_terms(sorted_q, sorted_new[:, :, 0], sorted_new[:, :, 1], causal, scale)
    global_peak = lax.pmax(partial_value[0], ("side", "seq"))
    factor = jnp.exp(partial_value[0] - global_peak)
    mass_sum, out_sum = lax.psum(
        (partial_value[1] * factor, partial_value[2] * factor[..., None]), ("side", "seq")
    )
    final_state = combine((global_peak, mass_sum, out_sum), own_part)
    attended_sorted = (
        (final_state[2] / final_state[1][..., None]).astype(jnp.bfloat16).reshape(row_count, -1)
    )
    attn_rows = jnp.dot(placing.T, attended_sorted, preferred_element_type=jnp.float32).astype(
        jnp.bfloat16
    )
    head_part = jnp.dot(attn_rows, w_out, preferred_element_type=jnp.float32)
    share_rows = row_count // lax.axis_size("tensor")
    row_start = lax.axis_index("tensor") * share_rows
    head_total = lax.psum(head_part, "tensor")
    attended_block = (head_total + raw_block.astype(jnp.float32)).astype(jnp.bfloat16)
    complete = lax.all_gather(attended_block, ("side", "seq"), axis=1, tiled=True)
    attended = lax.dynamic_slice_in_dim(attended_block, row_start, share_rows, 0)
    final_rows = rms_scale(complete, final_gain)
    logits = jnp.dot(final_rows, w_vocab, preferred_element_type=jnp.float32)
    vocab_here = logits.shape[1]
    offset = lax.axis_index(("side", "seq", "tensor")) * vocab_here
    matches = (offset + jnp.arange(vocab_here, dtype=jnp.int32))[None, :] == token_ids[:, None]
    picked = jnp.sum(jnp.where(matches, logits, 0.0), axis=1)
    row_peak = lax.pmax(jnp.max(logits, axis=1), ("side", "seq", "tensor"))
    exp_sum = jnp.sum(jnp.exp(logits - row_peak[:, None]), axis=1)
    exp_total, picked_total = lax.psum((exp_sum, picked), ("side", "seq", "tensor"))
    logprob = picked_total - row_peak - jnp.log(exp_total)
    return (attended, logprob)


def solution(mesh):
    in_specs = (
        P(("side", "seq"), None),
        P(),
        P(),
        P(("side", "seq"), "tensor"),
        P(("side", "seq"), None, "tensor"),
        P("tensor", ("side", "seq")),
        P(None, None, ("side", "seq"), "tensor"),
        P(None, ("side", "seq", "tensor")),
        P(),
        P(),
        P(),
    )
    out_specs = (P("tensor", ("side", "seq")), P())
    return jax.shard_map(
        per_device, mesh=mesh, in_specs=in_specs, out_specs=out_specs, check_vma=False
    )
```

profile of v0, /device:TPU:32, one launch (start us, length us, event | category | flops | bytes accessed | tf_op | source)
XLA Modules:
  0.0 738.2 jit_solution(13250182231077297181)
XLA Ops:
  8.0 1.1 fusion.46
  10.9 7.3 all-to-all-start
  19.0 1.2 reduce-window.6
  20.7 6.8 all-to-all-done
  27.9 1.8 copy.61
  32.6 113.6 %all-reduce.6.cloned.1.call-done = f32[512,8,128]{2,1,0:T(8,128)} async-done(((f32[512,8,128]{2,1,0:T(8,128)}), f32[512,8,128]{2,1,0:T(8,128)}) %all-reduce.6.cloned.1.call-update) | async-done | bytes 2097168 | tf_op jit(solution)/shard_map/psum | solution.py:112
  146.2 3.0 subtract_convert_fusion
  151.4 2.9 fusion.3
  154.3 4.2 bitcast_reduce_fusion
  158.5 1.5 copy-done.1
  160.0 127.1 %pmax.14 = f32[4,128,1,8]{1,3,0,2:T(8,128)S(1)} all-reduce(f32[4,128,1,8]{1,3,0,2:T(8,128)S(1)} %bitcast.214), channel_id=1, replica_groups=mesh['side'=2,'seq'=16,'tensor'=8] {'side','seq'}, use_global_device_ids=true, to_apply=%region_7.8 | all-reduce | flops 4096 | bytes 32768 | tf_op jit(solution)/shard_map/pmax | solution.py:144
  287.2 8.6 %fusion.14 = f32[4,128,1,8,128]{4,1,3,0,2:T(8,128)} fusion(f32[4,128,8,1024]{3,1,2,0:T(8,128)} %copy-done.1, f32[4,128,8]{1,2,0:T(8,128)S(1)} %get-tuple-element.25, pred[4,1024]{1,0:T(4,128)(4,1)S(1)} %broadcast_compare_fusion, f32[4,128,8]{1,2,0:T(8,128)S(1)} %get-tuple-element.20, bf16[2,4,1024,128]{3,2,1,0:T(8,128)(2,1)} %param.17), kind=kOutput, calls=%fused_computation.19 | convolution fusion | flops 1091043328 | bytes 19959808 | tf_op jit(solution)/shard_map/bskgp,bpkd->bskgd/dot_general | solution.py:62
  295.9 124.2 %psum.52 = f32[4,128,1,8]{1,3,0,2:T(8,128)S(1)} all-reduce(f32[4,128,1,8]{1,3,0,2:T(8,128)S(1)} %get-tuple-element.19), channel_id=1, replica_groups=mesh['side'=2,'seq'=16,'tensor'=8] {'side','seq'}, use_global_device_ids=true, to_apply=%region_12.13 | all-reduce | flops 4096 | bytes 32768 | tf_op jit(solution)/shard_map/psum | solution.py:146
  425.2 2.4 fusion.16
  428.7 2.1 fusion.25
  430.9 12.2 %all_to_all.32 = bf16[16,32,256]{2,0,1:T(8,128)(2,1)S(1)} all-to-all(bf16[16,32,256]{2,0,1:T(8,128)(2,1)S(1)} %bitcast.212), channel_id=1, replica_groups=mesh['side'=2,'seq'=16,'tensor'=8] {'side','seq'}, dimensions={1} | all-to-all | bytes 524288 | tf_op jit(solution)/shard_map/all_to_all | solution.py:97
  443.1 57.5 %all-reduce.8.cloned.1.call-done = f32[512,256]{1,0:T(8,128)} async-done(((f32[512,256]{1,0:T(8,128)}), f32[512,256]{1,0:T(8,128)}) %all-reduce.8.cloned.1.call-update) | async-done | bytes 524304 | tf_op jit(solution)/shard_map/psum | solution.py:159
  500.6 1.8 fusion.49
  502.5 1.4 constant_dynamic-slice_fusion
  503.9 62.5 %all-gather.2.cloned.1.call-done = bf16[512,8192]{1,0:T(8,128)(2,1)} async-done(((bf16[512,256]{1,0:T(8,128)(2,1)}), bf16[512,8192]{1,0:T(8,128)(2,1)}) %all-gather.2.cloned.1.call-update) | async-done | bytes 8388624 | tf_op jit(solution)/shard_map/all_gather | solution.py:161
  566.4 5.3 fusion
  572.2 8.5 %fusion.90 = (f32[512]{0:T(512)S(1)}, f32[512,594]{0,1:T(8,128)S(1)}) fusion(bf16[8192,594]{0,1:T(8,128)(2,1)} %param.18, bf16[512,8192]{1,0:T(8,128)(2,1)S(1)} %copy-done.2, f32[8192]{0:T(1024)S(1)} %convert_element_type.105, f32[512]{0:T(512)S(1)} %add_rsqrt_fusion), kind=kOutput, calls=%fused_computation.137 | convolution fusion | flops 4999913984 | bytes 19374080 | tf_op jit(solution)/shard_map/dot_general | solution.py:164
  580.7 76.0 %pmax.15 = f32[512]{0:T(512)S(1)} all-reduce(f32[512]{0:T(512)S(1)} %get-tuple-element.29), channel_id=1, replica_groups=mesh['side'=2,'seq'=16,'tensor'=8] {'side','seq','tensor'}, use_global_device_ids=true, to_apply=%region_19.20 | all-reduce | flops 512 | bytes 4096 | tf_op jit(solution)/shard_map/pmax | solution.py:169
  657.1 74.0 %all-reduce = (f32[512]{0:T(512)S(1)}, f32[512]{0:T(512)S(1)}) all-reduce(f32[512]{0:T(512)S(1)} %get-tuple-element.3, f32[512]{0:T(512)S(1)} %get-tuple-element.2), channel_id=1, replica_groups=mesh['side'=2,'seq'=16,'tensor'=8] {'side','seq','tensor'}, use_global_device_ids=true, to_apply=%region_21.22 | all-reduce | flops 1024 | bytes 8192 | tf_op jit(solution)/shard_map/psum | solution.py:171
  (70 shorter events, 16.9 us)
Async XLA Ops:
  7.2 20.3 %copy-start = (bf16[256,1024]{1,0:T(8,128)(2,1)S(1)}, bf16[256,1024]{1,0:T(8,128)(2,1)}, u32[]{:S(2)}) copy-start(bf16[256,1024]{1,0:T(8,128)(2,1)} %param.14) | copy-start | bytes 1572868
  10.9 16.6 %all-to-all-start = ((bf16[16,32,256]{2,0,1:T(8,128)(2,1)}), bf16[16,32,256]{2,0,1:T(8,128)(2,1)S(1)}, u32[]{:S(2)}, u32[]{:S(2)}) async-start(bf16[16,32,256]{2,0,1:T(8,128)(2,1)} %bitcast.200), calls=%async_computation | async-start | bytes 524288 | tf_op jit(solution)/shard_map/all_to_all | solution.py:98
  18.2 128.0 %all-reduce.6.cloned.1.call-start = ((), (), s32[]{:S(2)}) async-start(), calls=%async_computation.2 | async-start | bytes 4194304 | tf_op jit(solution)/shard_map/psum | solution.py:112
  29.7 0.7 copy-start.6
  29.7 0.7 copy-start.9
  29.7 1.8 copy-start.5
  29.7 390.4 %all-reduce.10.cloned.1.call-start = ((), (), s32[]{:S(2)}) async-start(), calls=%async_computation.5 | async-start | bytes 5242880 | tf_op jit(solution)/shard_map/psum | solution.py:146
  149.8 1.6 copy-start.4
  154.3 5.7 copy-start.1
  295.8 204.8 %all-reduce.8.cloned.1.call-start = ((), (), s32[]{:S(2)}) async-start(), calls=%async_computation.3 | async-start | bytes 1048576 | tf_op jit(solution)/shard_map/psum | solution.py:159
  423.6 1.6 copy-start.10
  427.6 1.0 copy-start.11
  428.7 2.2 copy-start.3
  430.8 71.7 %copy-start.7 = (bf16[8192]{0:T(1024)(128)(2,1)S(1)}, bf16[8192]{0:T(1024)(128)(2,1)}, u32[]{:S(2)}) copy-start(bf16[8192]{0:T(1024)(128)(2,1)} %param.13) | copy-start | bytes 49156
  430.8 135.6 %all-gather.2.cloned.1.call-start = ((), (), s32[]{:S(2)}) async-start(), calls=%async_computation.4 | async-start | bytes 8650752 | tf_op jit(solution)/shard_map/all_gather | solution.py:161
  566.4 5.8 copy-start.2
  572.2 84.6 %copy-start.8 = (s32[512]{0:T(512)S(1)}, s32[512]{0:T(512)}, u32[]{:S(2)}) copy-start(s32[512]{0:T(512)} %param.19) | copy-start | bytes 6148
Sparse Core Ops, SparseCore 0:
  29.8 116.3 all-reduce.5
  296.0 115.6 all-reduce.9
  430.9 69.6 all-reduce.7
  503.3 63.1 all-gather.1
where the time goes:
time: 740 us; the launch traced here: 738 us
  blocking collectives  414 us (56%)
  waiting for transfers between devices  241 us (33%)
  matrix products  27.6 us (4%)
  other arithmetic  23.1 us (3%)
  between operations  14.1 us (2%)
  local copies, waits for them, and re-layouts  11.7 us (2%)
  starting transfers between devices  7.49 us (1%)
    pmax x1, blocking collectives, per_device(): global_peak = lax.pmax(partial_value[0], ('side', 'seq'))  127 us
    psum x1, blocking collectives, per_device(): lax.psum((partial_value[1] * factor, partial_value[2] * factor[..., None]...  124 us
    psum x1, waiting for transfers between devices, per_device(): query_sum, pair_sum = lax.psum((query_part, pair_part), ('side', 'seq'))  114 us
    pmax x1, blocking collectives, per_device(): row_peak = lax.pmax(jnp.max(logits, axis=1), ('side', 'seq', 'tensor'))  76 us
    psum x1, blocking collectives, per_device(): lax.psum((exp_sum, picked), ('side', 'seq', 'tensor'))  74 us
    all_gather x1, waiting for transfers between devices, per_device(): lax.all_gather(attended_block, ('side', 'seq'), axis=1, tiled=True)  62.5 us
    psum x1, waiting for transfers between devices, per_device(): head_total = lax.psum(head_part, 'tensor')  57.5 us
  transfers between devices with their start and end apart: 5, of which 4 were waited for; matrix products, arithmetic and copies ran while one was open for 1% of the time, Pallas kernels for 0%

commit v1 on v0

v1 whole, which is shorter than its diff:
```python
import functools
import math

import jax
import jax.numpy as jnp
from jax import lax
from jax.experimental import pallas as pl
from jax.experimental.pallas import tpu as pltpu
from jax.sharding import PartitionSpec as P

HD = 128
TRAJ = 4
MESH = pl.DeviceIdType.MESH

epsilon = 1e-06
rope_base = 1000000.0
masked_low = -1e30
SCALE2 = float(HD) ** (-0.5) * math.log2(math.e)

F32 = jnp.float32
BF16 = jnp.bfloat16


def dot(a, b):
    return jnp.dot(a, b, preferred_element_type=F32)


def dot_nt(a, b):
    return lax.dot_general(a, b, (((1,), (1,)), ((), ())), preferred_element_type=F32)


def rows(start, size):
    return pl.ds(pl.multiple_of(start, size), size)


def column(row):
    return jnp.broadcast_to(row, (128, 128)).T


def merge(parts):
    top = functools.reduce(jnp.maximum, [p[1] for p in parts])
    factors = [jnp.exp2((p[1] - top) * SCALE2) for p in parts]
    mass = sum(p[2] * f for p, f in zip(parts, factors))
    outs = [
        sum(p[0](h) * f[:, h : h + 1] for p, f in zip(parts, factors)) for h in range(8)
    ]
    return outs, top, mass


def kernel(
    x_ref,
    ag_ref,
    fg_ref,
    wq_ref,
    wkv_ref,
    wo_hbm,
    kv_hbm,
    wv_hbm,
    tok_ref,
    clen_ref,
    traj_ref,
    cos_ref,
    sin_ref,
    att_ref,
    lp_ref,
    wo,
    kv,
    wv,
    nx,
    xn,
    raw,
    place,
    place_t,
    xs,
    part,
    r1,
    s2,
    r2,
    sum2,
    r3,
    qkv,
    o_all,
    ml_all,
    rc1,
    rm1,
    sc2,
    sm2,
    rc2,
    rm2,
    oc2,
    mc2,
    rc3,
    rm3,
    ho,
    hpb,
    zs,
    zr,
    feat,
    acc,
    st,
    zt,
    fs,
    fz,
    lsem,
    bsem,
    asem,
    rawr,
    p1r,
    p2r,
    p3r,
    g1r,
    g2r,
    g3r,
    c1r,
    c2r,
    c3r,
    h1r,
    h2r,
    h3r,
    zrr,
    zgr,
    ftr,
    fbr,
    ztr,
    fzr,
):
    c = lax.axis_index("side")
    s = lax.axis_index("seq")
    z = lax.axis_index("tensor")
    j = c * 16 + s
    along = lax.div(s, 4)
    across = lax.rem(s, 4)
    a = along + c * (across - along)
    b = across + c * (along - across)
    row0 = c * 256 + a * 64 + b * 16

    def seq_of(side, a_, b_):
        straight = a_ * 4 + b_
        return straight + side * (b_ * 4 + a_ - straight)

    def blk(a_, b_):
        return c * 16 + seq_of(c, a_, b_)

    def peer(a_, b_):
        return (c, seq_of(c, a_, b_), z)

    def turn(v, k):
        return lax.rem(v + k, 4)

    sib = (1 - c, s, z)

    def send(src, dst, ssem, rsem, dev):
        pltpu.make_async_remote_copy(
            src_ref=src, dst_ref=dst, send_sem=ssem, recv_sem=rsem, device_id=dev, device_id_type=MESH
        ).start()

    def wait(ref, sem):
        pltpu.make_async_copy(ref, ref, sem).wait()

    def local(src, dst, n):
        return pltpu.make_async_copy(src, dst, lsem.at[n])

    local(kv_hbm, kv, 0).start()
    local(wo_hbm, wo, 1).start()
    local(wv_hbm, wv, 2).start()

    barrier = pltpu.get_barrier_semaphore()

    def greet(k, carry):
        i = lax.rem(j + k, 32)
        pl.semaphore_signal(barrier, inc=1, device_id=(lax.div(i, 16), lax.rem(i, 16), z), device_id_type=MESH)
        return carry

    lax.fori_loop(1, 32, greet, 0)

    def greet_z(k, carry):
        pl.semaphore_signal(barrier, inc=1, device_id=(c, s, lax.rem(z + k, 8)), device_id_type=MESH)
        return carry

    lax.fori_loop(1, 8, greet_z, 0)

    total = jnp.zeros((16, 1), F32)
    for n in range(8):
        v = x_ref[:, n * 1024 : (n + 1) * 1024].astype(F32)
        total = total + jnp.sum(v * v, axis=1, keepdims=True)
    unit = lax.rsqrt(total * (1.0 / 8192.0) + epsilon)
    for n in range(8):
        cols = slice(n * 1024, (n + 1) * 1024)
        v = x_ref[:, cols].astype(F32)
        nx[:, cols] = (v * unit * ag_ref[:, cols].astype(F32)).astype(BF16)

    pl.semaphore_wait(barrier, 38)

    def send_rows(k, carry):
        i = lax.rem(j + k, 32)
        send(
            nx.at[:, rows(i * 256, 256)],
            xn.at[rows(j * 16, 16), :],
            bsem.at[0],
            asem.at[0],
            (lax.div(i, 16), lax.rem(i, 16), z),
        )
        return carry

    lax.fori_loop(1, 32, send_rows, 0)
    xn[rows(j * 16, 16), :] = nx[:, rows(j * 256, 256)]

    quarter = lax.rem(j, 4)
    holds_raw = lax.div(j, 4) == z

    @pl.when(holds_raw)
    def _():
        def send_raw(k, carry):
            i = lax.rem(j + k, 32)
            send(
                x_ref.at[:, rows(i * 256, 256)],
                raw.at[rows(quarter * 16, 16), :],
                bsem.at[1],
                rawr.at[quarter],
                (lax.div(i, 16), lax.rem(i, 16), z),
            )
            return carry

        lax.fori_loop(1, 32, send_raw, 0)
        raw[rows(quarter * 16, 16), :] = x_ref[:, rows(j * 256, 256)]

    traj = traj_ref[...].astype(F32)
    traj_cols = [column(traj[g : g + 1, :]) for g in range(4)]
    sub = lax.broadcasted_iota(jnp.int32, (128, 128), 0)
    lane = lax.broadcasted_iota(jnp.int32, (128, 128), 1)
    for g in range(4):
        step_col = jnp.zeros((128, 1), F32)
        step_row = jnp.zeros((1, 128), F32)
        for e in range(g + 1):
            same = jnp.where(traj_cols[g] == traj[e : e + 1, :], 1.0, 0.0)
            if e == g:
                same = jnp.where(lane < sub, same, 0.0)
            step_col = step_col + jnp.sum(same, axis=1, keepdims=True)
            same = jnp.where(traj_cols[e] == traj[g : g + 1, :], 1.0, 0.0)
            if e == g:
                same = jnp.where(sub < lane, same, 0.0)
            step_row = step_row + jnp.sum(same, axis=0, keepdims=True)
        slot_col = traj_cols[g] * 128.0 + step_col
        slot_row = traj[g : g + 1, :] * 128.0 + step_row
        for e in range(4):
            place_t[g * 128 : (g + 1) * 128, e * 128 : (e + 1) * 128] = jnp.where(
                (lane + e * 128).astype(F32) == slot_col, 1.0, 0.0
            ).astype(BF16)
            place[e * 128 : (e + 1) * 128, g * 128 : (g + 1) * 128] = jnp.where(
                (sub + e * 128).astype(F32) == slot_row, 1.0, 0.0
            ).astype(BF16)

    wait(xn.at[0:496], asem.at[0])

    def project(half):
        at = rows(half * 256, 256)
        xs[at, :] = dot(place[at, :], xn[...]).astype(BF16)
        part[at, 0:1024] = dot(xs[at, :], wq_ref[...])
        part[at, 1024:1280] = dot(xs[at, :], wkv_ref[...])

    project(1 - c)
    for k in (1, 2, 3, 0):
        q = turn(b, k)
        send(part.at[rows((1 - c) * 256 + q * 64, 64), :], r1.at[rows(q * 64, 64), :], bsem.at[2], p1r.at[q], sib)
    project(c)

    def pair_sum(q):
        wait(r1.at[rows(q * 64, 64), :], p1r.at[q])
        return part[rows(c * 256 + q * 64, 64), :] + r1[rows(q * 64, 64), :]

    for k in (1, 2, 3):
        q = turn(a, k)
        s2[q] = pair_sum(q).astype(BF16)
        send(s2.at[q], r2.at[a], bsem.at[3], p2r.at[a], peer(q, b))
    sum2[...] = pair_sum(a)
    for k in (3, 2, 1):
        q = turn(a, k)
        wait(r2.at[q], p2r.at[q])
        sum2[...] += r2[q].astype(F32)
    for k in (1, 2, 3):
        q = turn(b, k)
        send(sum2.at[rows(q * 16, 16), :], r3.at[b], bsem.at[4], p3r.at[b], peer(a, q))
    r3[b] = sum2[rows(b * 16, 16), :]
    for k in (3, 2, 1):
        q = turn(b, k)
        wait(r3.at[q], p3r.at[q])
    sums = (r3[0] + r3[1]) + (r3[2] + r3[3])
    cosine = cos_ref[...]
    sine = sin_ref[...]
    mine = rows(row0, 16)
    for h in range(9):
        v = sums[:, h * 128 : (h + 1) * 128]
        qkv[mine, h * 128 : (h + 1) * 128] = (v * cosine + pltpu.roll(v, 64, 1) * sine).astype(BF16)
    qkv[mine, 1152:1280] = sums[:, 1152:1280].astype(BF16)

    def spread(ref, n, r_b, r_a, r_s):
        for k in (1, 2, 3):
            send(ref.at[mine, :], ref.at[mine, :], bsem.at[n], r_b.at[b], peer(a, turn(b, k)))
        for k in (3, 2, 1):
            q = turn(b, k)
            wait(ref.at[rows(c * 256 + a * 64 + q * 16, 16), :], r_b.at[q])
        span = rows(c * 256 + a * 64, 64)
        for k in (1, 2, 3):
            send(ref.at[span, :], ref.at[span, :], bsem.at[n + 1], r_a.at[a], peer(turn(a, k), b))
        for k in (3, 2, 1):
            q = turn(a, k)
            wait(ref.at[rows(c * 256 + q * 64, 64), :], r_a.at[q])
        for n_half in (0, 1):
            span = rows(c * 256 + n_half * 128, 128)
            send(ref.at[span, :], ref.at[span, :], bsem.at[n + 2], r_s.at[n_half], sib)

    spread(qkv, 5, g1r, g2r, g3r)

    local(kv_hbm, kv, 0).wait()
    positions = j * 1024 + lax.broadcasted_iota(jnp.int32, (1, 1024), 1)

    def attend(t):
        at = rows(t * 128, 128)
        allowed = positions < clen_ref[t]
        keys = kv[0, t]
        values = kv[1, t]
        peaks = jnp.zeros((128, 128), F32)
        masses = jnp.zeros((128, 128), F32)
        for h in range(0, 8, 2):
            pair = jnp.concatenate(
                [qkv[at, h * 128 : (h + 1) * 128], qkv[at, (h + 1) * 128 : (h + 2) * 128]], axis=0
            )
            scores = jnp.where(allowed, dot_nt(pair, keys), masked_low)
            peak = jnp.max(scores, axis=1, keepdims=True)
            weights = jnp.exp2((scores - peak) * SCALE2)
            mass = jnp.sum(weights, axis=1, keepdims=True)
            out = dot(weights.astype(BF16), values)
            for e in (0, 1):
                o_all[at, (h + e) * 128 : (h + e + 1) * 128] = out[e * 128 : (e + 1) * 128]
                peaks = jnp.where(lane == h + e, peak[e * 128 : (e + 1) * 128], peaks)
                masses = jnp.where(lane == h + e, mass[e * 128 : (e + 1) * 128], masses)
        ml_all[0, at, :] = peaks
        ml_all[1, at, :] = masses

    def attend_own(n, carry):
        attend(c * 2 + n)
        return carry

    lax.fori_loop(0, 2, attend_own, 0)

    def attend_other(n, carry):
        t = (1 - c) * 2 + n
        wait(qkv.at[rows(t * 128, 128), :], g3r.at[n])
        attend(t)
        at = rows(t * 128, 128)
        to = rows(n * 128, 128)
        send(o_all.at[at, :], rc1.at[to, :], bsem.at[8], c1r.at[n], sib)
        send(ml_all.at[:, at, :], rm1.at[:, to, :], bsem.at[9], c1r.at[n + 2], sib)
        return carry

    lax.fori_loop(0, 2, attend_other, 0)

    def join_pair(q):
        at = rows(c * 256 + q * 64, 64)
        to = rows(q * 64, 64)
        return merge(
            [
                (lambda h: o_all[at, h * 128 : (h + 1) * 128], ml_all[0, at, :], ml_all[1, at, :]),
                (lambda h: rc1[to, h * 128 : (h + 1) * 128], rm1[0, to, :], rm1[1, to, :]),
            ]
        )

    for n in (0, 1):
        wait(rc1.at[rows(n * 128, 128), :], c1r.at[n])
        wait(rm1.at[:, rows(n * 128, 128), :], c1r.at[n + 2])
    for k in (1, 2, 3):
        q = turn(a, k)
        outs, top, mass = join_pair(q)
        for h in range(8):
            sc2[q, :, h * 128 : (h + 1) * 128] = outs[h].astype(BF16)
        sm2[q, 0] = top
        sm2[q, 1] = mass
        send(sc2.at[q], rc2.at[a], bsem.at[10], c2r.at[a], peer(q, b))
        send(sm2.at[q], rm2.at[a], bsem.at[11], c2r.at[a + 4], peer(q, b))
    outs, top, mass = join_pair(a)
    for h in range(8):
        oc2[:, h * 128 : (h + 1) * 128] = outs[h]
    mc2[0] = top
    mc2[1] = mass

    own_traj = lax.div(row0, 128)
    own_step = lax.rem(row0, 128)
    own_rows = rows(own_traj * 128, 128)
    own_q = jnp.concatenate([qkv[mine, h * 128 : (h + 1) * 128] for h in range(8)], axis=0)
    own_scores = dot_nt(own_q, qkv[own_rows, 1024:1152])
    own_scores = jnp.where(lane <= own_step + (sub & 15), own_scores, masked_low)
    own_peak = jnp.max(own_scores, axis=1, keepdims=True)
    own_weights = jnp.exp2((own_scores - own_peak) * SCALE2)
    own_mass = jnp.sum(own_weights, axis=1, keepdims=True)
    own_out = dot(own_weights.astype(BF16), qkv[own_rows, 1152:1280])
    own_peaks = jnp.zeros((16, 128), F32)
    own_masses = jnp.zeros((16, 128), F32)
    lane16 = lane[0:16]
    for h in range(8):
        own_peaks = jnp.where(lane16 == h, own_peak[h * 16 : (h + 1) * 16], own_peaks)
        own_masses = jnp.where(lane16 == h, own_mass[h * 16 : (h + 1) * 16], own_masses)

    def arrived(k):
        q = turn(a, k)
        wait(rc2.at[q], c2r.at[q])
        wait(rm2.at[q], c2r.at[q + 4])
        return (lambda h: rc2[q, :, h * 128 : (h + 1) * 128].astype(F32), rm2[q, 0], rm2[q, 1])

    parts = [(lambda h: oc2[:, h * 128 : (h + 1) * 128], mc2[0], mc2[1])]
    parts += [arrived(k) for k in (3, 2, 1)]
    outs, top, mass = merge(parts)
    for h in range(8):
        oc2[:, h * 128 : (h + 1) * 128] = outs[h]
    mc2[0] = top
    mc2[1] = mass
    for k in (1, 2, 3):
        q = turn(b, k)
        send(oc2.at[rows(q * 16, 16), :], rc3.at[b], bsem.at[12], c3r.at[b], peer(a, q))
        send(mc2.at[:, rows(q * 16, 16), :], rm3.at[b], bsem.at[13], c3r.at[b + 4], peer(a, q))
    rc3[b] = oc2[rows(b * 16, 16), :]
    rm3[b] = mc2[:, rows(b * 16, 16), :]
    for k in (3, 2, 1):
        q = turn(b, k)
        wait(rc3.at[q], c3r.at[q])
        wait(rm3.at[q], c3r.at[q + 4])
    parts = [(lambda h, q=q: rc3[q, :, h * 128 : (h + 1) * 128], rm3[q, 0], rm3[q, 1]) for q in range(4)]
    parts.append((lambda h: own_out[h * 16 : (h + 1) * 16], own_peaks, own_masses))
    outs, top, mass = merge(parts)
    for h in range(8):
        ho[mine, h * 128 : (h + 1) * 128] = (outs[h] / mass[:, h : h + 1]).astype(BF16)

    spread(ho, 14, h1r, h2r, h3r)

    local(wo_hbm, wo, 1).wait()
    own_half = rows(c * 256, 256)
    hpb[own_half, :] = dot(ho[own_half, :], wo[...]).astype(BF16)
    for n in (0, 1):
        wait(ho.at[rows((1 - c) * 256 + n * 128, 128), :], h3r.at[n])
    other_half = rows((1 - c) * 256, 256)
    hpb[other_half, :] = dot(ho[other_half, :], wo[...]).astype(BF16)

    def send_z(k, carry):
        q = lax.rem(z + k, 8)
        zs[q] = dot(place_t[rows(q * 64, 64), :], hpb[...]).astype(BF16)
        send(zs.at[q], zr.at[z], bsem.at[17], zrr.at[z], (c, s, q))
        return carry

    lax.fori_loop(1, 8, send_z, 0)
    total = dot(place_t[rows(z * 64, 64), :], hpb[...])
    for m in range(4):

        @pl.when(z * 4 + m != j)
        def _():
            wait(raw.at[rows(m * 16, 16), :], rawr.at[m])

    total = total + raw[...].astype(F32)
    for k in range(1, 8):
        q = lax.rem(z + 8 - k, 8)
        wait(zr.at[q], zrr.at[q])
        total = total + zr[q].astype(F32)
    attended = total.astype(BF16)
    att_ref[...] = attended
    attended = attended.astype(F32)
    my_z = rows(z * 64, 64)
    feat[j, my_z, :] = (attended * fg_ref[:, rows(j * 256, 256)].astype(F32)).astype(BF16)

    def send_feat_z(k, carry):
        send(feat.at[j, my_z, :], feat.at[j, my_z, :], bsem.at[18], zgr.at[z], (c, s, lax.rem(z + k, 8)))
        return carry

    lax.fori_loop(1, 8, send_feat_z, 0)

    squares = jnp.sum(attended * attended, axis=1, keepdims=True)
    squares = jnp.concatenate([jnp.broadcast_to(squares, (64, 128))] * 2, axis=0).T
    st[j] = squares[0:8]

    def send_squares(k, carry):
        i = lax.rem(j + k, 32)
        send(st.at[j], st.at[j], bsem.at[19], asem.at[1], (lax.div(i, 16), lax.rem(i, 16), z))
        return carry

    local(wv_hbm, wv, 2).wait()

    def multiply(i, first=False):
        def half(n, carry):
            at = rows(n * 256, 256)
            product = dot(feat[i, at, :], wv[rows(i * 256, 256), :])
            if first:
                acc[at, :] = product
            else:
                acc[at, :] += product
            return carry

        lax.fori_loop(0, 2, half, 0)

    def send_block(i, dev):
        send(feat.at[i], feat.at[i], bsem.at[20], ftr.at[i], dev)

    def send_top(i, dev):
        send(feat.at[i, 0:256, :], feat.at[i, 0:256, :], bsem.at[20], ftr.at[i], dev)

    def send_bottom(i, dev):
        send(feat.at[i, 256:512, :], feat.at[i, 256:512, :], bsem.at[20], fbr.at[i], dev)

    def wait_halves(i):
        wait(feat.at[i, 0:256, :], ftr.at[i])
        wait(feat.at[i, 256:512, :], fbr.at[i])

    a_up, a_down, a_far = turn(a, 1), turn(a, 3), turn(a, 2)
    b_up, b_down, b_far = turn(b, 1), turn(b, 3), turn(b, 2)

    def fan(i):
        send_block(i, peer(a_up, b))
        send_block(i, peer(a_down, b))
        send_block(i, sib)

    for k in range(1, 8):
        q = lax.rem(z + 8 - k, 8)
        wait(feat.at[j, rows(q * 64, 64), :], zgr.at[q])
    send_block(j, peer(a, b_up))
    send_block(j, peer(a, b_down))
    fan(j)
    lax.fori_loop(1, 32, send_squares, 0)
    multiply(j, first=True)
    i = blk(a, b_down)
    wait(feat.at[i], ftr.at[i])
    send_top(i, peer(a, b_up))
    fan(i)
    i = blk(a, b_up)
    wait(feat.at[i], ftr.at[i])
    send_bottom(i, peer(a, b_down))
    fan(i)

    wait(st.at[0:31], asem.at[1])
    sum_sq = st[0]
    for n in range(1, 32):
        sum_sq = sum_sq + st[n]
    zt[z] = sum_sq

    def send_sum_sq(k, carry):
        send(zt.at[z], zt.at[z], bsem.at[21], ztr.at[z], (c, s, lax.rem(z + k, 8)))
        return carry

    lax.fori_loop(1, 8, send_sum_sq, 0)

    i = blk(a, b_far)
    wait_halves(i)
    fan(i)

    def b_order(b_, n):
        step = jnp.where(n == 0, 0, jnp.where(n == 1, 3, n - 1))
        return lax.rem(b_ + step, 4)

    def sib_blk(a_, b_):
        return (1 - c) * 16 + seq_of(1 - c, a_, b_)

    def take(i):
        wait(feat.at[i], ftr.at[i])
        multiply(i)

    def near(n, carry):
        bn = b_order(b, n)
        i = blk(a_down, bn)
        wait(feat.at[i], ftr.at[i])
        send_top(i, peer(a_up, b))
        send_block(i, sib)
        k = blk(a_up, bn)
        wait(feat.at[k], ftr.at[k])
        send_bottom(k, peer(a_down, b))
        send_block(k, sib)

        @pl.when(n > 0)
        def _():
            multiply(blk(a, bn))

        take(sib_blk(b, b_order(a, n)))
        return carry

    lax.fori_loop(0, 4, near, 0)

    def far(n, carry):
        bn = b_order(b, n)
        i = blk(a_far, bn)
        wait_halves(i)
        send_block(i, sib)
        multiply(blk(a_down, bn))
        multiply(blk(a_up, bn))
        multiply(i)
        sn = b_order(a, n)
        take(sib_blk(turn(b, 3), sn))
        take(sib_blk(turn(b, 1), sn))
        return carry

    lax.fori_loop(0, 4, far, 0)

    def last(n, carry):
        take(sib_blk(turn(b, 2), b_order(a, n)))
        return carry

    lax.fori_loop(0, 4, last, 0)

    for k in range(1, 8):
        q = lax.rem(z + 8 - k, 8)
        wait(zt.at[q], ztr.at[q])
    entries = acc.shape[1]
    offset = (j * 8 + z) * entries
    entry = (offset + lax.broadcasted_iota(jnp.int32, (1, entries), 1)).astype(F32)
    token = tok_ref[...].astype(F32)
    for g in range(4):
        root = []
        for q in (2 * g, 2 * g + 1):
            root.append(column(lax.rsqrt(zt[q][0:1] * (1.0 / 8192.0) + epsilon))[0:64, 0:1])
        logits = acc[g * 128 : (g + 1) * 128, :] * jnp.concatenate(root, axis=0)
        token_col = column(token[g : g + 1, :])[:, 0:1]
        picked = jnp.sum(jnp.where(entry == token_col, logits, 0.0), axis=1, keepdims=True)
        peak = jnp.max(logits, axis=1, keepdims=True)
        exp_sum = jnp.sum(jnp.exp(logits - peak), axis=1, keepdims=True)
        flat = jnp.where(lane == 0, peak, jnp.where(lane == 1, exp_sum, picked)).T
        for n in range(3):
            fs[j, n * 4 + g : n * 4 + g + 1, :] = flat[n : n + 1]
    fs[j, 12:16, :] = jnp.zeros((4, 128), F32)

    def send_stats(k, carry):
        i = lax.rem(j + k, 32)
        send(fs.at[j], fs.at[j], bsem.at[22], asem.at[2], (lax.div(i, 16), lax.rem(i, 16), z))
        return carry

    lax.fori_loop(1, 32, send_stats, 0)

    def join_stats(ref, count):
        top = ref[0, 0:4, :]
        for n in range(1, count):
            top = jnp.maximum(top, ref[n, 0:4, :])
        exp_total = jnp.zeros((4, 128), F32)
        picked_total = jnp.zeros((4, 128), F32)
        for n in range(count):
            exp_total = exp_total + ref[n, 4:8, :] * jnp.exp(ref[n, 0:4, :] - top)
            picked_total = picked_total + ref[n, 8:12, :]
        return top, exp_total, picked_total

    wait(fs.at[0:31], asem.at[2])
    top, exp_total, picked_total = join_stats(fs, 32)
    fz[z, 0:4, :] = top
    fz[z, 4:8, :] = exp_total
    fz[z, 8:12, :] = picked_total
    fz[z, 12:16, :] = jnp.zeros((4, 128), F32)

    def send_final(k, carry):
        send(fz.at[z], fz.at[z], bsem.at[23], fzr.at[z], (c, s, lax.rem(z + k, 8)))
        return carry

    lax.fori_loop(1, 8, send_final, 0)
    for k in range(1, 8):
        q = lax.rem(z + 8 - k, 8)
        wait(fz.at[q], fzr.at[q])
    top, exp_total, picked_total = join_stats(fz, 8)
    lp_ref[...] = picked_total - top - jnp.log(exp_total)

    wait(xn.at[0:496], bsem.at[0])

    @pl.when(holds_raw)
    def _():
        wait(xn.at[0:496], bsem.at[1])

    wait(r1, bsem.at[2])
    wait(r2.at[0:3], bsem.at[3])
    wait(r3.at[0:3], bsem.at[4])
    for ref, n in ((qkv, 5), (ho, 14)):
        wait(ref.at[0:48], bsem.at[n])
        wait(ref.at[0:192], bsem.at[n + 1])
        wait(ref.at[0:256], bsem.at[n + 2])
    wait(rc1, bsem.at[8])
    wait(rm1, bsem.at[9])
    wait(rc2.at[0:3], bsem.at[10])
    wait(rm2.at[0:3], bsem.at[11])
    wait(rc3.at[0:3], bsem.at[12])
    wait(rm3.at[0:3], bsem.at[13])
    wait(zr.at[0:7], bsem.at[17])
    wait(zr.at[0:7], bsem.at[18])
    wait(st.at[0:31], bsem.at[19])
    wait(feat.at[0:31], bsem.at[20])
    wait(zt.at[0:7], bsem.at[21])
    wait(fs.at[0:31], bsem.at[22])
    wait(fz.at[0:7], bsem.at[23])


def rope_tables(cache_len):
    side = lax.axis_index("side")
    seq = lax.axis_index("seq")
    along, across = seq // 4, seq % 4
    a = along + side * (across - along)
    b = across + side * (along - across)
    row0 = side * 256 + a * 64 + b * 16
    half_dim = HD // 2
    mine = jnp.sum(jnp.where(jnp.arange(TRAJ) == row0 // 128, cache_len, 0))
    places = mine + row0 % 128 + jnp.arange(16, dtype=jnp.int32)
    spread = jnp.exp(
        jnp.arange(half_dim).astype(F32) * (-2.0 * math.log(rope_base) / HD)
    )
    angles = places.astype(F32)[:, None] * spread[None, :]
    cosine = jnp.cos(angles)
    sine = jnp.sin(angles)
    return (
        jnp.concatenate([cosine, cosine], axis=1),
        jnp.concatenate([-sine, sine], axis=1),
    )


def per_device(
    x_rows,
    attn_gain,
    final_gain,
    w_query,
    w_kv,
    w_out,
    kv_cache,
    w_vocab,
    token_ids,
    cache_len,
    row_traj,
):
    cosine, sine = rope_tables(cache_len)
    entries = w_vocab.shape[1]
    vmem = pl.BlockSpec(memory_space=pltpu.VMEM)
    smem = pl.BlockSpec(memory_space=pltpu.SMEM)
    hbm = pl.BlockSpec(memory_space=pl.ANY)
    dma = pltpu.SemaphoreType.DMA
    attended, logprob = pl.pallas_call(
        kernel,
        out_shape=(
            jax.ShapeDtypeStruct((64, 256), BF16),
            jax.ShapeDtypeStruct((4, 128), F32),
        ),
        in_specs=[vmem, vmem, vmem, vmem, vmem, hbm, hbm, hbm, vmem, smem, vmem, vmem, vmem],
        out_specs=(vmem, vmem),
        scratch_shapes=[
            pltpu.VMEM((1024, 256), BF16),
            pltpu.VMEM((2, 4, 1024, 128), BF16),
            pltpu.VMEM((8192, entries), BF16),
            pltpu.VMEM((16, 8192), BF16),
            pltpu.VMEM((512, 256), BF16),
            pltpu.VMEM((64, 256), BF16),
            pltpu.VMEM((512, 512), BF16),
            pltpu.VMEM((512, 512), BF16),
            pltpu.VMEM((512, 256), BF16),
            pltpu.VMEM((512, 1280), F32),
            pltpu.VMEM((256, 1280), F32),
            pltpu.VMEM((4, 64, 1280), BF16),
            pltpu.VMEM((4, 64, 1280), BF16),
            pltpu.VMEM((64, 1280), F32),
            pltpu.VMEM((4, 16, 1280), F32),
            pltpu.VMEM((512, 1280), BF16),
            pltpu.VMEM((512, 1024), F32),
            pltpu.VMEM((2, 512, 128), F32),
            pltpu.VMEM((256, 1024), F32),
            pltpu.VMEM((2, 256, 128), F32),
            pltpu.VMEM((4, 64, 1024), BF16),
            pltpu.VMEM((4, 2, 64, 128), F32),
            pltpu.VMEM((4, 64, 1024), BF16),
            pltpu.VMEM((4, 2, 64, 128), F32),
            pltpu.VMEM((64, 1024), F32),
            pltpu.VMEM((2, 64, 128), F32),
            pltpu.VMEM((4, 16, 1024), F32),
            pltpu.VMEM((4, 2, 16, 128), F32),
            pltpu.VMEM((512, 1024), BF16),
            pltpu.VMEM((512, 256), BF16),
            pltpu.VMEM((8, 64, 256), BF16),
            pltpu.VMEM((8, 64, 256), BF16),
            pltpu.VMEM((32, 512, 256), BF16),
            pltpu.VMEM((512, entries), F32),
            pltpu.VMEM((32, 8, 128), F32),
            pltpu.VMEM((8, 8, 128), F32),
            pltpu.VMEM((32, 16, 128), F32),
            pltpu.VMEM((8, 16, 128), F32),
            dma((3,)),
            dma((24,)),
            dma((3,)),
            dma((4,)),
            dma((4,)),
            dma((4,)),
            dma((4,)),
            dma((4,)),
            dma((4,)),
            dma((2,)),
            dma((4,)),
            dma((8,)),
            dma((8,)),
            dma((4,)),
            dma((4,)),
            dma((2,)),
            dma((8,)),
            dma((8,)),
            dma((32,)),
            dma((32,)),
            dma((8,)),
            dma((8,)),
        ],
        compiler_params=pltpu.CompilerParams(
            collective_id=0, has_side_effects=True, vmem_limit_bytes=60 * 1024 * 1024
        ),
        cost_estimate=pl.CostEstimate(
            flops=8_000_000_000, bytes_accessed=14_000_000, transcendentals=5_000_000
        ),
    )(
        x_rows,
        attn_gain.reshape(1, -1),
        final_gain.reshape(1, -1),
        w_query,
        w_kv.reshape(w_kv.shape[0], -1),
        w_out,
        kv_cache,
        w_vocab,
        token_ids.reshape(4, 128),
        cache_len,
        row_traj.reshape(4, 128),
        cosine,
        sine,
    )
    return attended, logprob.reshape(-1)


def solution(mesh):
    in_specs = (
        P(("side", "seq"), None),
        P(),
        P(),
        P(("side", "seq"), "tensor"),
        P(("side", "seq"), None, "tensor"),
        P("tensor", ("side", "seq")),
        P(None, None, ("side", "seq"), "tensor"),
        P(None, ("side", "seq", "tensor")),
        P(),
        P(),
        P(),
    )
    out_specs = (P("tensor", ("side", "seq")), P())
    return jax.shard_map(
        per_device, mesh=mesh, in_specs=in_specs, out_specs=out_specs, check_vma=False
    )
```

time: 740 us -> 167 us (0.23)
  blocking collectives: 414 us -> 0 us
  waiting for transfers between devices: 241 us -> 0 us
  Pallas kernels: 0 us -> 141 us
  matrix products: 27.6 us -> 0 us
  other arithmetic: 23.1 us -> 2.11 us
  between operations: 14.1 us -> 1.37 us
  local copies, waits for them, and re-layouts: 11.7 us -> 21 us
  starting transfers between devices: 7.49 us -> 0 us
    pmax x2 -> x0, blocking collectives: 203 us -> none  [the longest x1 127 us: per_device(): global_peak = lax.pmax(partial_value[0], ('side', 'seq'))]
    psum x2 -> x0, blocking collectives: 198 us -> none  [the longest x1 124 us: per_device(): lax.psum((partial_value[1] * factor, partial_value[2] * factor[..., None]...]
    psum x3 -> x0, waiting for transfers between devices: 171 us -> none  [the longest x1 114 us: per_device(): query_sum, pair_sum = lax.psum((query_part, pair_part), ('side', 'seq'))]
    pallas_call x0 -> x1, Pallas kernels: none -> 141 us  [per_device(): pl.pallas_call(kernel, out_shape=(jax.ShapeDtypeStruct((64, 256), BF16),...]
    all_gather x1 -> x0, waiting for transfers between devices: 62.5 us -> none  [per_device(): lax.all_gather(attended_block, ('side', 'seq'), axis=1, tiled=True)]
    dot_general x10 -> x0, matrix products: 27.6 us -> none  [the longest x2 11.1 us: block_terms(): jnp.einsum('bskgp,bpkd->bskgd', weights.astype(jnp.bfloat16), values_bloc...]
    all_to_all x1 -> x0, blocking collectives: 12.2 us -> none  [per_device(): lax.all_to_all(x_rows, ('side', 'seq'), split_axis=1, concat_axis=0, tile...]
    unnamed x27 -> x4, local copies, waits for them, and re-layouts: 6.33 us -> 18.3 us
  transfers between devices with their start and end apart: 5 -> 0, of which waited for: 4 -> 0; matrix products, arithmetic and copies ran while one was open for 1% -> 0% of each run, Pallas kernels for 0% -> 0%
where the time goes in v1:
time: 167 us; the launch traced here: 165 us
  Pallas kernels  141 us (84%)
  local copies, waits for them, and re-layouts  21 us (13%)
  other arithmetic  2.11 us (1%)
    pallas_call x1, Pallas kernels, per_device(): pl.pallas_call(kernel, out_shape=(jax.ShapeDtypeStruct((64, 256), BF16),...  141 us
    unnamed x4, local copies, waits for them, and re-layouts  18.3 us

profile of v1, /device:TPU:32, one launch (start us, length us, event | category | flops | bytes accessed | tf_op | source)
XLA Modules:
  0.0 165.5 jit_solution(575566445802415490)
XLA Ops:
  0.7 1.3 fusion.1
  2.7 0.1 fusion
  2.8 0.7 pad_maximum_fusion
  3.5 1.3 reshape.33.ag_ref
  4.8 1.4 reshape.34.fg_ref
  6.2 1.6 copy.16
  7.7 14.1 %copy.13.wv_hbm = bf16[8192,594]{1,0:T(8,128)(2,1)} copy(bf16[8192,594]{0,1:T(8,128)(2,1)} %param.18) | data formatting | bytes 19464192 | tf_op args[7]
  21.9 141.0 %shard_map.122 = (bf16[64,256]{1,0:T(8,128)(2,1)}, f32[4,128]{1,0:T(4,128)}) custom-call(bf16[16,8192]{1,0:T(8,128)(2,1)} %x_ref.1, bf16[1,8192]{1,0:T(2,128)(2,1)} %reshape.33.ag_ref, bf16[1,8192]{1,0:T(2,128)(2,1)} %reshape.34.fg_ref, bf16[256,1024]{1,0:T(8,128)(2,1)} %wq_ref.1, bf16[256,256]{1,0:T(8,128)(2,1)} %bitcast.8, bf16[1024,256]{1,0:T(8,128)(2,1)} %wo_hbm.1, ...), custom_call_target="tpu_custom_call" | custom-call | flops 8000000000 | bytes 14000000 | tf_op jit(solution)/shard_map/pallas_call | solution.py:728
  162.9 1.4 copy.19
  164.3 1.2 copy.20
  (2 shorter events, 0.0 us)

commit v2 on v1

--- a/solution.py
+++ b/solution.py
@@ -3,6 +3,7 @@
 
 import jax
 import jax.numpy as jnp
+import numpy as np
 from jax import lax
 from jax.experimental import pallas as pl
 from jax.experimental.pallas import tpu as pltpu
@@ -31,6 +32,10 @@
 
 def rows(start, size):
     return pl.ds(pl.multiple_of(start, size), size)
+
+
+def span(start, size, unit):
+    return pl.ds(pl.multiple_of(start, unit), size)
 
 
 def column(row):
@@ -51,7 +56,7 @@
     x_ref,
     ag_ref,
     fg_ref,
-    wq_ref,
+    wq_hbm,
     wkv_ref,
     wo_hbm,
     kv_hbm,
@@ -59,12 +64,13 @@
     tok_ref,
     clen_ref,
     traj_ref,
-    cos_ref,
-    sin_ref,
+    spread_ref,
     att_ref,
     lp_ref,
+    wq,
     wo,
-    kv,
+    keys,
+    values,
     wv,
     nx,
     xn,
@@ -96,7 +102,9 @@
     zs,
     zr,
     feat,
+    tail,
     acc,
+    flat,
     st,
     zt,
     fs,
@@ -121,6 +129,11 @@
     zgr,
     ftr,
     fbr,
+    qbr,
+    qar,
+    qur,
+    qdr,
+    qsr,
     ztr,
     fzr,
 ):
@@ -138,9 +151,6 @@
         straight = a_ * 4 + b_
         return straight + side * (b_ * 4 + a_ - straight)
 
-    def blk(a_, b_):
-        return c * 16 + seq_of(c, a_, b_)
-
     def peer(a_, b_):
         return (c, seq_of(c, a_, b_), z)
 
@@ -160,9 +170,15 @@
     def local(src, dst, n):
         return pltpu.make_async_copy(src, dst, lsem.at[n])
 
-    local(kv_hbm, kv, 0).start()
-    local(wo_hbm, wo, 1).start()
-    local(wv_hbm, wv, 2).start()
+    copies = [
+        local(wq_hbm, wq, 0),
+        local(kv_hbm.at[0], keys.at[:, :, 0:128], 1),
+        local(kv_hbm.at[1], values.at[:, :, 0:128], 2),
+        local(wo_hbm, wo, 3),
+        local(wv_hbm, wv, 4),
+    ]
+    for copy in copies:
+        copy.start()
 
     barrier = pltpu.get_barrier_semaphore()
 
@@ -184,10 +200,10 @@
         v = x_ref[:, n * 1024 : (n + 1) * 1024].astype(F32)
         total = total + jnp.sum(v * v, axis=1, keepdims=True)
     unit = lax.rsqrt(total * (1.0 / 8192.0) + epsilon)
-    for n in range(8):
-        cols = slice(n * 1024, (n + 1) * 1024)
+    for n in range(64):
+        cols = slice(n * 128, (n + 1) * 128)
         v = x_ref[:, cols].astype(F32)
-        nx[:, cols] = (v * unit * ag_ref[:, cols].astype(F32)).astype(BF16)
+        nx[:, cols] = (v * unit * ag_ref[n : n + 1, :].astype(F32)).astype(BF16)
 
     pl.semaphore_wait(barrier, 38)
 
@@ -250,13 +266,34 @@
                 (sub + e * 128).astype(F32) == slot_row, 1.0, 0.0
             ).astype(BF16)
 
+    key_place = j * 1024 + lax.broadcasted_iota(jnp.int32, (1024, 128), 0)
+    first_lane = lax.broadcasted_iota(jnp.int32, (1024, 128), 1) == 0
+    for t in range(4):
+        past = jnp.logical_and(first_lane, key_place >= clen_ref[t])
+        keys[t, :, 128:256] = jnp.where(past, masked_low, 0.0).astype(BF16)
+        values[t, :, 128:256] = jnp.ones((1024, 128), BF16)
+    acc[...] = jnp.zeros(acc.shape, F32)
+
+    own_traj = lax.div(row0, 128)
+    own_step = lax.rem(row0, 128)
+    cached = clen_ref[0]
+    for t in range(1, 4):
+        cached = jnp.where(own_traj == t, clen_ref[t], cached)
+    lane16 = lane[0:16]
+    angles = (cached + own_step + sub[0:16]).astype(F32) * spread_ref[...]
+    cosine = jnp.cos(angles)
+    sine = jnp.sin(angles)
+    sine = jnp.where(lane16 < 64, -sine, sine)
+
+    copies[0].wait()
     wait(xn.at[0:496], asem.at[0])
 
     def project(half):
         at = rows(half * 256, 256)
         xs[at, :] = dot(place[at, :], xn[...]).astype(BF16)
-        part[at, 0:1024] = dot(xs[at, :], wq_ref[...])
-        part[at, 1024:1280] = dot(xs[at, :], wkv_ref[...])
+        part[at, 0:1024] = dot(xs[at, :], wq[...])
+        part[at, 1024:1152] = dot(xs[at, :], wkv_ref[:, 0, :])
+        part[at, 1152:1280] = dot(xs[at, :], wkv_ref[:, 1, :])
 
     project(1 - c)
     for k in (1, 2, 3, 0):
@@ -285,8 +322,6 @@
         q = turn(b, k)
         wait(r3.at[q], p3r.at[q])
     sums = (r3[0] + r3[1]) + (r3[2] + r3[3])
-    cosine = cos_ref[...]
-    sine = sin_ref[...]
     mine = rows(row0, 16)
     for h in range(9):
         v = sums[:, h * 128 : (h + 1) * 128]
@@ -299,92 +334,90 @@
         for k in (3, 2, 1):
             q = turn(b, k)
             wait(ref.at[rows(c * 256 + a * 64 + q * 16, 16), :], r_b.at[q])
-        span = rows(c * 256 + a * 64, 64)
+        at = rows(c * 256 + a * 64, 64)
         for k in (1, 2, 3):
-            send(ref.at[span, :], ref.at[span, :], bsem.at[n + 1], r_a.at[a], peer(turn(a, k), b))
+            send(ref.at[at, :], ref.at[at, :], bsem.at[n + 1], r_a.at[a], peer(turn(a, k), b))
         for k in (3, 2, 1):
             q = turn(a, k)
             wait(ref.at[rows(c * 256 + q * 64, 64), :], r_a.at[q])
         for n_half in (0, 1):
-            span = rows(c * 256 + n_half * 128, 128)
-            send(ref.at[span, :], ref.at[span, :], bsem.at[n + 2], r_s.at[n_half], sib)
+            at = rows(c * 256 + n_half * 128, 128)
+            send(ref.at[at, :], ref.at[at, :], bsem.at[n + 2], r_s.at[n_half], sib)
 
     spread(qkv, 5, g1r, g2r, g3r)
 
-    local(kv_hbm, kv, 0).wait()
-    positions = j * 1024 + lax.broadcasted_iota(jnp.int32, (1, 1024), 1)
+    copies[1].wait()
+    copies[2].wait()
+    one = jnp.where(lax.broadcasted_iota(jnp.int32, (512, 128), 1) == 0, 1.0, 0.0).astype(BF16)
 
     def attend(t):
         at = rows(t * 128, 128)
-        allowed = positions < clen_ref[t]
-        keys = kv[0, t]
-        values = kv[1, t]
         peaks = jnp.zeros((128, 128), F32)
         masses = jnp.zeros((128, 128), F32)
-        for h in range(0, 8, 2):
-            pair = jnp.concatenate(
-                [qkv[at, h * 128 : (h + 1) * 128], qkv[at, (h + 1) * 128 : (h + 2) * 128]], axis=0
+        for h in range(0, 8, 4):
+            heads = jnp.concatenate(
+                [qkv[at, (h + e) * 128 : (h + e + 1) * 128] for e in range(4)], axis=0
             )
-            scores = jnp.where(allowed, dot_nt(pair, keys), masked_low)
+            scores = dot_nt(jnp.concatenate([heads, one], axis=1), keys[t])
             peak = jnp.max(scores, axis=1, keepdims=True)
-            weights = jnp.exp2((scores - peak) * SCALE2)
-            mass = jnp.sum(weights, axis=1, keepdims=True)
-            out = dot(weights.astype(BF16), values)
-            for e in (0, 1):
-                o_all[at, (h + e) * 128 : (h + e + 1) * 128] = out[e * 128 : (e + 1) * 128]
-                peaks = jnp.where(lane == h + e, peak[e * 128 : (e + 1) * 128], peaks)
-                masses = jnp.where(lane == h + e, mass[e * 128 : (e + 1) * 128], masses)
+            weights = jnp.exp2((scores - peak) * SCALE2).astype(BF16)
+            out = dot(weights, values[t])
+            for e in range(4):
+                part_rows = slice(e * 128, (e + 1) * 128)
+                o_all[at, (h + e) * 128 : (h + e + 1) * 128] = out[part_rows, 0:128]
+                peaks = jnp.where(lane == h + e, peak[part_rows], peaks)
+                masses = jnp.where(lane == h + e, out[part_rows, 128:256], masses)
         ml_all[0, at, :] = peaks
         ml_all[1, at, :] = masses
 
-    def attend_own(n, carry):
-        attend(c * 2 + n)
-        return carry
-
-    lax.fori_loop(0, 2, attend_own, 0)
-
     def attend_other(n, carry):
         t = (1 - c) * 2 + n
-        wait(qkv.at[rows(t * 128, 128), :], g3r.at[n])
+        at = rows(t * 128, 128)
+        wait(qkv.at[at, :], g3r.at[n])
         attend(t)
-        at = rows(t * 128, 128)
         to = rows(n * 128, 128)
         send(o_all.at[at, :], rc1.at[to, :], bsem.at[8], c1r.at[n], sib)
         send(ml_all.at[:, at, :], rm1.at[:, to, :], bsem.at[9], c1r.at[n + 2], sib)
         return carry
 
-    lax.fori_loop(0, 2, attend_other, 0)
-
     def join_pair(q):
         at = rows(c * 256 + q * 64, 64)
-        to = rows(q * 64, 64)
-        return merge(
+        to = slice(q * 64, (q + 1) * 64)
+        outs, top, mass = merge(
             [
                 (lambda h: o_all[at, h * 128 : (h + 1) * 128], ml_all[0, at, :], ml_all[1, at, :]),
                 (lambda h: rc1[to, h * 128 : (h + 1) * 128], rm1[0, to, :], rm1[1, to, :]),
             ]
         )
 
-    for n in (0, 1):
-        wait(rc1.at[rows(n * 128, 128), :], c1r.at[n])
-        wait(rm1.at[:, rows(n * 128, 128), :], c1r.at[n + 2])
-    for k in (1, 2, 3):
-        q = turn(a, k)
-        outs, top, mass = join_pair(q)
-        for h in range(8):
-            sc2[q, :, h * 128 : (h + 1) * 128] = outs[h].astype(BF16)
-        sm2[q, 0] = top
-        sm2[q, 1] = mass
-        send(sc2.at[q], rc2.at[a], bsem.at[10], c2r.at[a], peer(q, b))
-        send(sm2.at[q], rm2.at[a], bsem.at[11], c2r.at[a + 4], peer(q, b))
-    outs, top, mass = join_pair(a)
-    for h in range(8):
-        oc2[:, h * 128 : (h + 1) * 128] = outs[h]
-    mc2[0] = top
-    mc2[1] = mass
-
-    own_traj = lax.div(row0, 128)
-    own_step = lax.rem(row0, 128)
+        @pl.when(q != a)
+        def _():
+            for h in range(8):
+                sc2[q, :, h * 128 : (h + 1) * 128] = outs[h].astype(BF16)
+            sm2[q, 0] = top
+            sm2[q, 1] = mass
+            send(sc2.at[q], rc2.at[a], bsem.at[10], c2r.at[a], peer(q, b))
+            send(sm2.at[q], rm2.at[a], bsem.at[11], c2r.at[a + 4], peer(q, b))
+
+        @pl.when(q == a)
+        def _():
+            for h in range(8):
+                oc2[:, h * 128 : (h + 1) * 128] = outs[h]
+            mc2[0] = top
+            mc2[1] = mass
+
+    attend(c * 2)
+    lax.fori_loop(0, 2, attend_other, 0)
+    wait(rc1.at[0:128, :], c1r.at[0])
+    wait(rm1.at[:, 0:128, :], c1r.at[2])
+    join_pair(0)
+    join_pair(1)
+    attend(c * 2 + 1)
+    wait(rc1.at[128:256, :], c1r.at[1])
+    wait(rm1.at[:, 128:256, :], c1r.at[3])
+    join_pair(2)
+    join_pair(3)
+
     own_rows = rows(own_traj * 128, 128)
     own_q = jnp.concatenate([qkv[mine, h * 128 : (h + 1) * 128] for h in range(8)], axis=0)
     own_scores = dot_nt(own_q, qkv[own_rows, 1024:1152])
@@ -395,7 +428,6 @@
     own_out = dot(own_weights.astype(BF16), qkv[own_rows, 1152:1280])
     own_peaks = jnp.zeros((16, 128), F32)
     own_masses = jnp.zeros((16, 128), F32)
-    lane16 = lane[0:16]
     for h in range(8):
         own_peaks = jnp.where(lane16 == h, own_peak[h * 16 : (h + 1) * 16], own_peaks)
         own_masses = jnp.where(lane16 == h, own_mass[h * 16 : (h + 1) * 16], own_masses)
@@ -431,7 +463,7 @@
 
     spread(ho, 14, h1r, h2r, h3r)
 
-    local(wo_hbm, wo, 1).wait()
+    copies[3].wait()
     own_half = rows(c * 256, 256)
     hpb[own_half, :] = dot(ho[own_half, :], wo[...]).astype(BF16)
     for n in (0, 1):
@@ -439,13 +471,20 @@
     other_half = rows((1 - c) * 256, 256)
     hpb[other_half, :] = dot(ho[other_half, :], wo[...]).astype(BF16)
 
-    def send_z(k, carry):
+    zs[...] = dot(place_t[...], hpb[...]).astype(BF16)
+
+    def send_z_tail(k, carry):
         q = lax.rem(z + k, 8)
-        zs[q] = dot(place_t[rows(q * 64, 64), :], hpb[...]).astype(BF16)
-        send(zs.at[q], zr.at[z], bsem.at[17], zrr.at[z], (c, s, q))
-        return carry
-
-    lax.fori_loop(1, 8, send_z, 0)
+        send(zs.at[span(q * 64 + 48, 16, 16), :], zr.at[z, 48:64, :], bsem.at[17], zrr.at[z], (c, s, q))
+        return carry
+
+    def send_z_head(k, carry):
+        q = lax.rem(z + k, 8)
+        send(zs.at[span(q * 64, 48, 16), :], zr.at[z, 0:48, :], bsem.at[18], zrr.at[z + 8], (c, s, q))
+        return carry
+
+    lax.fori_loop(1, 8, send_z_tail, 0)
+    lax.fori_loop(1, 8, send_z_head, 0)
     total = dot(place_t[rows(z * 64, 64), :], hpb[...])
     for m in range(4):
 
@@ -454,80 +493,133 @@
             wait(raw.at[rows(m * 16, 16), :], rawr.at[m])
 
     total = total + raw[...].astype(F32)
+    gains = fg_ref[...].astype(F32)
+    gain_row = lax.broadcasted_iota(jnp.int32, (64, 128), 0)
+    gain = jnp.concatenate(
+        [jnp.sum(jnp.where(gain_row == 2 * j + n, gains, 0.0), axis=0, keepdims=True) for n in (0, 1)],
+        axis=1,
+    )
+
+    def block_of(a_, b_):
+        return c * 16 + a_ * 4 + b_
+
+    here = block_of(a, b)
+    tail_z = rows(z * 16, 16)
+    head_z = span(z * 48, 48, 16)
+    a_up, a_down, a_far = turn(a, 1), turn(a, 3), turn(a, 2)
+    b_up, b_down, b_far = turn(b, 1), turn(b, 3), turn(b, 2)
+    z_up = (c, s, lax.rem(z + 1, 8))
+    z_down = (c, s, lax.rem(z + 7, 8))
+
+    attended = total[48:64]
     for k in range(1, 8):
         q = lax.rem(z + 8 - k, 8)
-        wait(zr.at[q], zrr.at[q])
-        total = total + zr[q].astype(F32)
-    attended = total.astype(BF16)
-    att_ref[...] = attended
-    attended = attended.astype(F32)
-    my_z = rows(z * 64, 64)
-    feat[j, my_z, :] = (attended * fg_ref[:, rows(j * 256, 256)].astype(F32)).astype(BF16)
+        wait(zr.at[q, 48:64, :], zrr.at[q])
+        attended = attended + zr[q, 48:64, :].astype(F32)
+    attended = attended.astype(BF16)
+    att_ref[48:64, :] = attended
+    tail[here, tail_z, :] = (attended.astype(F32) * gain).astype(BF16)
+    for k in (1, 2, 3):
+        ref = tail.at[here, tail_z, :]
+        send(ref, ref, bsem.at[19], qbr.at[b], peer(a, turn(b, k)))
+
+    attended = total[0:48]
+    for k in range(1, 8):
+        q = lax.rem(z + 8 - k, 8)
+        wait(zr.at[q, 0:48, :], zrr.at[q + 8])
+        attended = attended + zr[q, 0:48, :].astype(F32)
+    attended = attended.astype(BF16)
+    att_ref[0:48, :] = attended
+    feat[here, head_z, :] = (attended.astype(F32) * gain).astype(BF16)
 
     def send_feat_z(k, carry):
-        send(feat.at[j, my_z, :], feat.at[j, my_z, :], bsem.at[18], zgr.at[z], (c, s, lax.rem(z + k, 8)))
+        ref = feat.at[here, head_z, :]
+        send(ref, ref, bsem.at[20], zgr.at[z], (c, s, lax.rem(z + k, 8)))
         return carry
 
     lax.fori_loop(1, 8, send_feat_z, 0)
 
-    squares = jnp.sum(attended * attended, axis=1, keepdims=True)
+    def send_chunk(q):
+        chunk = feat.at[here, span(q * 48, 48, 16), :]
+        for dev in (peer(a_up, b), peer(a_down, b), peer(a, b_up), peer(a, b_down), sib):
+            send(chunk, chunk, bsem.at[21], ftr.at[here], dev)
+
+    def pass_chunk(k, carry):
+        q = lax.rem(z + jnp.where(lax.rem(k, 2) == 1, lax.div(k + 1, 2), 8 - lax.div(k, 2)), 8)
+        wait(feat.at[here, span(q * 48, 48, 16), :], zgr.at[q])
+        send_chunk(q)
+        return carry
+
+    send_chunk(z)
+
+    for k in (3, 2, 1):
+        q = turn(b, k)
+        wait(tail.at[block_of(a, q), tail_z, :], qbr.at[q])
+    for k in (1, 2, 3):
+        ref = tail.at[pl.ds(block_of(a, 0), 4), tail_z, :]
+        send(ref, ref, bsem.at[22], qar.at[a], peer(turn(a, k), b))
+
+    squares = att_ref[...].astype(F32)
+    squares = jnp.sum(squares * squares, axis=1, keepdims=True)
     squares = jnp.concatenate([jnp.broadcast_to(squares, (64, 128))] * 2, axis=0).T
     st[j] = squares[0:8]
 
     def send_squares(k, carry):
         i = lax.rem(j + k, 32)
-        send(st.at[j], st.at[j], bsem.at[19], asem.at[1], (lax.div(i, 16), lax.rem(i, 16), z))
-        return carry
-
-    local(wv_hbm, wv, 2).wait()
-
-    def multiply(i, first=False):
-        def half(n, carry):
-            at = rows(n * 256, 256)
-            product = dot(feat[i, at, :], wv[rows(i * 256, 256), :])
-            if first:
-                acc[at, :] = product
-            else:
-                acc[at, :] += product
-            return carry
-
-        lax.fori_loop(0, 2, half, 0)
+        send(st.at[j], st.at[j], bsem.at[23], asem.at[1], (lax.div(i, 16), lax.rem(i, 16), z))
+        return carry
+
+    lax.fori_loop(1, 3, pass_chunk, 0)
+
+    def tail_of(q):
+        return tail.at[pl.ds(c * 16, 16), rows(q * 16, 16), :]
+
+    for k in (3, 2, 1):
+        q = turn(a, k)
+        wait(tail.at[pl.ds(block_of(q, 0), 4), tail_z, :], qar.at[q])
+    send(tail_of(z), tail_of(z), bsem.at[24], qur.at[1], z_up)
+    send(tail_of(z), tail_of(z), bsem.at[24], qdr.at[1], z_down)
+    send(tail_of(z), tail_of(z), bsem.at[24], qsr.at[z], sib)
+
+    lax.fori_loop(3, 8, pass_chunk, 0)
+    lax.fori_loop(1, 32, send_squares, 0)
+    copies[4].wait()
+
+    def multiply(*blocks):
+        acc[0:384, :] += sum(
+            dot_nt(feat[side * 16 + a_ * 4 + b_], wv[:, rows(side * 4096 + seq_of(side, a_, b_) * 256, 256)])
+            for side, a_, b_ in blocks
+        )
 
     def send_block(i, dev):
-        send(feat.at[i], feat.at[i], bsem.at[20], ftr.at[i], dev)
+        send(feat.at[i], feat.at[i], bsem.at[21], ftr.at[i], dev)
 
     def send_top(i, dev):
-        send(feat.at[i, 0:256, :], feat.at[i, 0:256, :], bsem.at[20], ftr.at[i], dev)
+        ref = feat.at[i, 0:192, :]
+        send(ref, ref, bsem.at[21], ftr.at[i], dev)
 
     def send_bottom(i, dev):
-        send(feat.at[i, 256:512, :], feat.at[i, 256:512, :], bsem.at[20], fbr.at[i], dev)
+        ref = feat.at[i, 192:384, :]
+        send(ref, ref, bsem.at[21], fbr.at[i], dev)
+
+    def wait_block(i):
+        wait(feat.at[i], ftr.at[i])
 
     def wait_halves(i):
-        wait(feat.at[i, 0:256, :], ftr.at[i])
-        wait(feat.at[i, 256:512, :], fbr.at[i])
-
-    a_up, a_down, a_far = turn(a, 1), turn(a, 3), turn(a, 2)
-    b_up, b_down, b_far = turn(b, 1), turn(b, 3), turn(b, 2)
+        wait(feat.at[i, 0:192, :], ftr.at[i])
+        wait(feat.at[i, 192:384, :], fbr.at[i])
 
     def fan(i):
         send_block(i, peer(a_up, b))
         send_block(i, peer(a_down, b))
         send_block(i, sib)
 
-    for k in range(1, 8):
-        q = lax.rem(z + 8 - k, 8)
-        wait(feat.at[j, rows(q * 64, 64), :], zgr.at[q])
-    send_block(j, peer(a, b_up))
-    send_block(j, peer(a, b_down))
-    fan(j)
-    lax.fori_loop(1, 32, send_squares, 0)
-    multiply(j, first=True)
-    i = blk(a, b_down)
-    wait(feat.at[i], ftr.at[i])
+    i = block_of(a, b_down)
+    wait_block(i)
     send_top(i, peer(a, b_up))
     fan(i)
-    i = blk(a, b_up)
-    wait(feat.at[i], ftr.at[i])
+    i = block_of(a, b_up)
+    wait_block(i)
     send_bottom(i, peer(a, b_down))
     fan(i)
 
@@ -538,66 +630,84 @@
     zt[z] = sum_sq
 
     def send_sum_sq(k, carry):
-        send(zt.at[z], zt.at[z], bsem.at[21], ztr.at[z], (c, s, lax.rem(z + k, 8)))
+        send(zt.at[z], zt.at[z], bsem.at[25], ztr.at[z], (c, s, lax.rem(z + k, 8)))
         return carry
 
     lax.fori_loop(1, 8, send_sum_sq, 0)
 
-    i = blk(a, b_far)
+    i = block_of(a, b_far)
     wait_halves(i)
     fan(i)
 
-    def b_order(b_, n):
+    def order(b_, n):
         step = jnp.where(n == 0, 0, jnp.where(n == 1, 3, n - 1))
         return lax.rem(b_ + step, 4)
 
-    def sib_blk(a_, b_):
-        return (1 - c) * 16 + seq_of(1 - c, a_, b_)
-
-    def take(i):
-        wait(feat.at[i], ftr.at[i])
-        multiply(i)
+    def from_sib(a_, b_):
+        wait_block((1 - c) * 16 + a_ * 4 + b_)
+        return (1 - c, a_, b_)
 
     def near(n, carry):
-        bn = b_order(b, n)
-        i = blk(a_down, bn)
-        wait(feat.at[i], ftr.at[i])
+        bn = order(b, n)
+        i = block_of(a_down, bn)
+        wait_block(i)
         send_top(i, peer(a_up, b))
         send_block(i, sib)
-        k = blk(a_up, bn)
-        wait(feat.at[k], ftr.at[k])
-        send_bottom(k, peer(a_down, b))
-        send_block(k, sib)
-
-        @pl.when(n > 0)
+        i = block_of(a_up, bn)
+        wait_block(i)
+        send_bottom(i, peer(a_down, b))
+        send_block(i, sib)
+
+        q = lax.rem(z + 7 - n, 8)
+        wait(tail_of(q), qur.at[n + 1])
+        send(tail_of(q), tail_of(q), bsem.at[24], qsr.at[q], sib)
+
+        @pl.when(n < 3)
         def _():
-            multiply(blk(a, bn))
-
-        take(sib_blk(b, b_order(a, n)))
+            send(tail_of(q), tail_of(q), bsem.at[24], qur.at[n + 2], z_up)
+            p = lax.rem(z + 1 + n, 8)
+            wait(tail_of(p), qdr.at[n + 1])
+            send(tail_of(p), tail_of(p), bsem.at[24], qsr.at[p], sib)
+
+            @pl.when(n < 2)
+            def _():
+                send(tail_of(p), tail_of(p), bsem.at[24], qdr.at[n + 2], z_down)
+
+        multiply((c, a, bn), (c, a_down, bn), (c, a_up, bn), from_sib(b, order(a, n)))
         return carry
 
     lax.fori_loop(0, 4, near, 0)
 
     def far(n, carry):
-        bn = b_order(b, n)
-        i = blk(a_far, bn)
+        bn = order(b, n)
+        i = block_of(a_far, bn)
         wait_halves(i)
         send_block(i, sib)
-        multiply(blk(a_down, bn))
-        multiply(blk(a_up, bn))
-        multiply(i)
-        sn = b_order(a, n)
-        take(sib_blk(turn(b, 3), sn))
-        take(sib_blk(turn(b, 1), sn))
+        sn = order(a, n)
+        multiply((c, a_far, bn), from_sib(b_down, sn), from_sib(b_up, sn))
         return carry
 
     lax.fori_loop(0, 4, far, 0)
 
+    for n in range(8):
+        wait(tail.at[pl.ds((1 - c) * 16, 16), n * 16 : (n + 1) * 16, :], qsr.at[n])
+
+    def multiply_tail(n, carry):
+        side = lax.div(n, 4)
+        a_ = lax.rem(n, 4)
+        acc[384:512, :] += sum(
+            dot_nt(tail[n * 4 + b_], wv[:, rows(side * 4096 + seq_of(side, a_, b_) * 256, 256)])
+            for b_ in range(4)
+        )
+        return carry
+
+    lax.fori_loop(0, 8, multiply_tail, 0)
+
     def last(n, carry):
-        take(sib_blk(turn(b, 2), b_order(a, n)))
-        return carry
-
-    lax.fori_loop(0, 4, last, 0)
+        multiply(*[from_sib(b_far, order(a, 2 * n + e)) for e in (0, 1)])
+        return carry
+
+    lax.fori_loop(0, 2, last, 0)
 
     for k in range(1, 8):
         q = lax.rem(z + 8 - k, 8)
@@ -606,23 +716,34 @@
     offset = (j * 8 + z) * entries
     entry = (offset + lax.broadcasted_iota(jnp.int32, (1, entries), 1)).astype(F32)
     token = tok_ref[...].astype(F32)
+    roots = [column(lax.rsqrt(zt[q][0:1] * (1.0 / 8192.0) + epsilon))[0:64] for q in range(8)]
+    token_cols = [column(token[g : g + 1, :]) for g in range(4)]
+    tokens = [token_cols[q // 2][(q % 2) * 64 : (q % 2) * 64 + 64] for q in range(8)]
+
+    def regroup(cols):
+        return jnp.concatenate([v[0:48] for v in cols] + [v[48:64] for v in cols], axis=0)
+
+    roots = regroup(roots)
+    tokens = regroup(tokens)
     for g in range(4):
-        root = []
-        for q in (2 * g, 2 * g + 1):
-            root.append(column(lax.rsqrt(zt[q][0:1] * (1.0 / 8192.0) + epsilon))[0:64, 0:1])
-        logits = acc[g * 128 : (g + 1) * 128, :] * jnp.concatenate(root, axis=0)
-        token_col = column(token[g : g + 1, :])[:, 0:1]
-        picked = jnp.sum(jnp.where(entry == token_col, logits, 0.0), axis=1, keepdims=True)
+        at = slice(g * 128, (g + 1) * 128)
+        logits = acc[at, :] * roots[at, 0:1]
+        picked = jnp.sum(jnp.where(entry == tokens[at, 0:1], logits, 0.0), axis=1, keepdims=True)
         peak = jnp.max(logits, axis=1, keepdims=True)
         exp_sum = jnp.sum(jnp.exp(logits - peak), axis=1, keepdims=True)
-        flat = jnp.where(lane == 0, peak, jnp.where(lane == 1, exp_sum, picked)).T
+        flat[at, :] = jnp.where(lane == 0, peak, jnp.where(lane == 1, exp_sum, picked))
+    for g in range(4):
+        pieces = []
+        for q in (2 * g, 2 * g + 1):
+            pieces += [flat[q * 48 : (q + 1) * 48, :], flat[384 + q * 16 : 400 + q * 16, :]]
+        stats = jnp.concatenate(pieces, axis=0).T
         for n in range(3):
-            fs[j, n * 4 + g : n * 4 + g + 1, :] = flat[n : n + 1]
+            fs[j, n * 4 + g : n * 4 + g + 1, :] = stats[n : n + 1]
     fs[j, 12:16, :] = jnp.zeros((4, 128), F32)
 
     def send_stats(k, carry):
         i = lax.rem(j + k, 32)
-        send(fs.at[j], fs.at[j], bsem.at[22], asem.at[2], (lax.div(i, 16), lax.rem(i, 16), z))
+        send(fs.at[j], fs.at[j], bsem.at[26], asem.at[2], (lax.div(i, 16), lax.rem(i, 16), z))
         return carry
 
     lax.fori_loop(1, 32, send_stats, 0)
@@ -646,7 +767,7 @@
     fz[z, 12:16, :] = jnp.zeros((4, 128), F32)
 
     def send_final(k, carry):
-        send(fz.at[z], fz.at[z], bsem.at[23], fzr.at[z], (c, s, lax.rem(z + k, 8)))
+        send(fz.at[z], fz.at[z], bsem.at[27], fzr.at[z], (c, s, lax.rem(z + k, 8)))
         return carry
 
     lax.fori_loop(1, 8, send_final, 0)
@@ -675,35 +796,17 @@
     wait(rm2.at[0:3], bsem.at[11])
     wait(rc3.at[0:3], bsem.at[12])
     wait(rm3.at[0:3], bsem.at[13])
-    wait(zr.at[0:7], bsem.at[17])
-    wait(zr.at[0:7], bsem.at[18])
-    wait(st.at[0:31], bsem.at[19])
-    wait(feat.at[0:31], bsem.at[20])
-    wait(zt.at[0:7], bsem.at[21])
-    wait(fs.at[0:31], bsem.at[22])
-    wait(fz.at[0:7], bsem.at[23])
-
-
-def rope_tables(cache_len):
-    side = lax.axis_index("side")
-    seq = lax.axis_index("seq")
-    along, across = seq // 4, seq % 4
-    a = along + side * (across - along)
-    b = across + side * (along - across)
-    row0 = side * 256 + a * 64 + b * 16
-    half_dim = HD // 2
-    mine = jnp.sum(jnp.where(jnp.arange(TRAJ) == row0 // 128, cache_len, 0))
-    places = mine + row0 % 128 + jnp.arange(16, dtype=jnp.int32)
-    spread = jnp.exp(
-        jnp.arange(half_dim).astype(F32) * (-2.0 * math.log(rope_base) / HD)
-    )
-    angles = places.astype(F32)[:, None] * spread[None, :]
-    cosine = jnp.cos(angles)
-    sine = jnp.sin(angles)
-    return (
-        jnp.concatenate([cosine, cosine], axis=1),
-        jnp.concatenate([-sine, sine], axis=1),
-    )
+    wait(zs.at[0:112], bsem.at[17])
+    wait(zs.at[0:336], bsem.at[18])
+    wait(tail.at[0, 0:48, :], bsem.at[19])
+    wait(feat.at[0, 0:336, :], bsem.at[20])
+    wait(feat.at[0:31], bsem.at[21])
+    wait(feat.at[0, 0:192, :], bsem.at[22])
+    wait(st.at[0:31], bsem.at[23])
+    wait(tail.at[0:30], bsem.at[24])
+    wait(zt.at[0:7], bsem.at[25])
+    wait(fs.at[0:31], bsem.at[26])
+    wait(fz.at[0:7], bsem.at[27])
 
 
 def per_device(
@@ -719,8 +822,8 @@
     cache_len,
     row_traj,
 ):
-    cosine, sine = rope_tables(cache_len)
     entries = w_vocab.shape[1]
+    spread = np.exp(np.arange(HD // 2) * (-2.0 * math.log(rope_base) / HD)).astype(np.float32)
     vmem = pl.BlockSpec(memory_space=pltpu.VMEM)
     smem = pl.BlockSpec(memory_space=pltpu.SMEM)
     hbm = pl.BlockSpec(memory_space=pl.ANY)
@@ -731,12 +834,14 @@
             jax.ShapeDtypeStruct((64, 256), BF16),
             jax.ShapeDtypeStruct((4, 128), F32),
         ),
-        in_specs=[vmem, vmem, vmem, vmem, vmem, hbm, hbm, hbm, vmem, smem, vmem, vmem, vmem],
+        in_specs=[vmem, vmem, vmem, hbm, vmem, hbm, hbm, hbm, vmem, smem, vmem, vmem],
         out_specs=(vmem, vmem),
         scratch_shapes=[
+            pltpu.VMEM((256, 1024), BF16),
             pltpu.VMEM((1024, 256), BF16),
-            pltpu.VMEM((2, 4, 1024, 128), BF16),
-            pltpu.VMEM((8192, entries), BF16),
+            pltpu.VMEM((4, 1024, 256), BF16),
+            pltpu.VMEM((4, 1024, 256), BF16),
+            pltpu.VMEM((entries, 8192), BF16),
             pltpu.VMEM((16, 8192), BF16),
             pltpu.VMEM((512, 256), BF16),
             pltpu.VMEM((64, 256), BF16),
@@ -764,16 +869,18 @@
             pltpu.VMEM((4, 2, 16, 128), F32),
             pltpu.VMEM((512, 1024), BF16),
             pltpu.VMEM((512, 256), BF16),
+            pltpu.VMEM((512, 256), BF16),
             pltpu.VMEM((8, 64, 256), BF16),
-            pltpu.VMEM((8, 64, 256), BF16),
-            pltpu.VMEM((32, 512, 256), BF16),
+            pltpu.VMEM((32, 384, 256), BF16),
+            pltpu.VMEM((32, 128, 256), BF16),
             pltpu.VMEM((512, entries), F32),
+            pltpu.VMEM((512, 128), F32),
             pltpu.VMEM((32, 8, 128), F32),
             pltpu.VMEM((8, 8, 128), F32),
             pltpu.VMEM((32, 16, 128), F32),
             pltpu.VMEM((8, 16, 128), F32),
-            dma((3,)),
-            dma((24,)),
+            dma((5,)),
+            dma((28,)),
             dma((3,)),
             dma((4,)),
             dma((4,)),
@@ -788,10 +895,15 @@
             dma((4,)),
             dma((4,)),
             dma((2,)),
-            dma((8,)),
+            dma((16,)),
             dma((8,)),
             dma((32,)),
             dma((32,)),
+            dma((4,)),
+            dma((4,)),
+            dma((5,)),
+            dma((5,)),
+            dma((8,)),
             dma((8,)),
             dma((8,)),
         ],
@@ -803,18 +915,17 @@
         ),
     )(
         x_rows,
-        attn_gain.reshape(1, -1),
-        final_gain.reshape(1, -1),
+        attn_gain.reshape(64, 128),
+        final_gain.reshape(64, 128),
         w_query,
-        w_kv.reshape(w_kv.shape[0], -1),
+        w_kv,
         w_out,
         kv_cache,
-        w_vocab,
+        w_vocab.T,
         token_ids.reshape(4, 128),
         cache_len,
         row_traj.reshape(4, 128),
-        cosine,
-        sine,
+        jnp.asarray(np.concatenate([spread, spread])[None]),
     )
     return attended, logprob.reshape(-1)
 

time: 167 us -> 144 us (0.86)
  local copies, waits for them, and re-layouts: 21 us -> 2.62 us
  other arithmetic: 2.11 us -> 0 us
    unnamed x4 -> x2, local copies, waits for them, and re-layouts: 18.3 us -> 2.62 us
    reshape x2 -> x0, local copies, waits for them, and re-layouts: 2.7 us -> none  [the longest x1 1.35 us: per_device(): final_gain.reshape(1, -1)]
where the time goes in v2:
time: 144 us
  Pallas kernels  141 us (98%)
  local copies, waits for them, and re-layouts  2.62 us (2%)
    pallas_call x1, Pallas kernels, per_device(): pl.pallas_call(kernel, out_shape=(jax.ShapeDtypeStruct((64, 256), BF16),...  141 us

profile of v2, /device:TPU:32, one launch (start us, length us, event | category | flops | bytes accessed | tf_op | source)
XLA Modules:
  0.0 144.0 jit_solution(14304587442225032673)
XLA Ops:
  0.6 140.8 %shard_map.131 = (bf16[64,256]{1,0:T(8,128)(2,1)}, f32[4,128]{1,0:T(4,128)}) custom-call(bf16[16,8192]{1,0:T(8,128)(2,1)} %x_ref.1, bf16[64,128]{1,0:T(8,128)(2,1)} %bitcast.8, bf16[64,128]{1,0:T(8,128)(2,1)} %bitcast.9, bf16[256,1024]{1,0:T(8,128)(2,1)} %wq_hbm.1, bf16[256,2,128]{2,1,0:T(2,128)(2,1)} %wkv_ref.1, bf16[1024,256]{1,0:T(8,128)(2,1)} %wo_hbm.1, ...), custom_call_target="tpu_custom_call" | custom-call | flops 8000000000 | bytes 14000000 | tf_op jit(solution)/shard_map/pallas_call | solution.py:831
  141.4 1.4 copy.16
  142.8 1.2 copy.17

commit v3 on v1

v3 whole, which is shorter than its diff:
```python
import functools
import math

import jax
import jax.numpy as jnp
import numpy as np
from jax import lax
from jax.experimental import pallas as pl
from jax.experimental.pallas import tpu as pltpu
from jax.sharding import PartitionSpec as P

HD = 128
TRAJ = 4
MESH = pl.DeviceIdType.MESH

epsilon = 1e-06
rope_base = 1000000.0
masked_low = -1e30
SCALE2 = float(HD) ** (-0.5) * math.log2(math.e)

F32 = jnp.float32
BF16 = jnp.bfloat16


def dot(a, b):
    return jnp.dot(a, b, preferred_element_type=F32)


def dot_nt(a, b):
    return lax.dot_general(a, b, (((1,), (1,)), ((), ())), preferred_element_type=F32)


def rows(start, size):
    return pl.ds(pl.multiple_of(start, size), size)


def column(row):
    return jnp.broadcast_to(row, (128, 128)).T


def merge(parts):
    top = functools.reduce(jnp.maximum, [p[1] for p in parts])
    factors = [jnp.exp2((p[1] - top) * SCALE2) for p in parts]
    mass = sum(p[2] * f for p, f in zip(parts, factors))
    outs = [
        sum(p[0](h) * f[:, h : h + 1] for p, f in zip(parts, factors)) for h in range(8)
    ]
    return outs, top, mass


def kernel(
    x_ref,
    ag_ref,
    fg_ref,
    wq_hbm,
    wkv_ref,
    wo_hbm,
    kv_hbm,
    wv_hbm,
    tok_ref,
    clen_ref,
    traj_ref,
    spread_ref,
    att_ref,
    lp_ref,
    wq,
    wo,
    keys,
    keys_t,
    values,
    wv,
    nx,
    xn,
    raw,
    place,
    place_t,
    xs,
    part,
    r1,
    s2,
    r2,
    sum2,
    r3,
    qkv,
    o_all,
    ml_all,
    rc1,
    rm1,
    sc2,
    sm2,
    rc2,
    rm2,
    oc2,
    mc2,
    rc3,
    rm3,
    ho,
    hpb,
    zs,
    zr,
    gz,
    feat,
    acc,
    st,
    zt,
    fs,
    lsem,
    bsem,
    asem,
    rawr,
    p1r,
    p2r,
    p3r,
    g1r,
    g2r,
    g3r,
    c1r,
    c2r,
    c3r,
    h1r,
    h2r,
    h3r,
    zrr,
    zgr,
    ftr,
    fbr,
    ztr,
    fsr,
):
    c = lax.axis_index("side")
    s = lax.axis_index("seq")
    z = lax.axis_index("tensor")
    j = c * 16 + s
    along = lax.div(s, 4)
    across = lax.rem(s, 4)
    a = along + c * (across - along)
    b = across + c * (along - across)
    row0 = c * 256 + a * 64 + b * 16

    def seq_of(side, a_, b_):
        straight = a_ * 4 + b_
        return straight + side * (b_ * 4 + a_ - straight)

    def blk(a_, b_):
        return c * 16 + seq_of(c, a_, b_)

    def peer(a_, b_):
        return (c, seq_of(c, a_, b_), z)

    def turn(v, k):
        return lax.rem(v + k, 4)

    sib = (1 - c, s, z)

    def send(src, dst, ssem, rsem, dev):
        pltpu.make_async_remote_copy(
            src_ref=src, dst_ref=dst, send_sem=ssem, recv_sem=rsem, device_id=dev, device_id_type=MESH
        ).start()

    def wait(ref, sem):
        pltpu.make_async_copy(ref, ref, sem).wait()

    def local(src, dst, n):
        return pltpu.make_async_copy(src, dst, lsem.at[n])

    copies = [
        local(wq_hbm, wq, 0),
        local(kv_hbm.at[0], keys, 1),
        local(kv_hbm.at[1], values.at[:, :, 0:128], 2),
        local(wo_hbm, wo, 3),
        local(wv_hbm, wv, 4),
    ]
    for copy in copies:
        copy.start()

    barrier = pltpu.get_barrier_semaphore()

    def greet(k, carry):
        i = lax.rem(j + k, 32)
        pl.semaphore_signal(barrier, inc=1, device_id=(lax.div(i, 16), lax.rem(i, 16), z), device_id_type=MESH)
        return carry

    lax.fori_loop(1, 32, greet, 0)

    def greet_z(k, carry):
        pl.semaphore_signal(barrier, inc=1, device_id=(c, s, lax.rem(z + k, 8)), device_id_type=MESH)
        return carry

    lax.fori_loop(1, 8, greet_z, 0)

    total = jnp.zeros((16, 1), F32)
    for n in range(8):
        v = x_ref[:, n * 1024 : (n + 1) * 1024].astype(F32)
        total = total + jnp.sum(v * v, axis=1, keepdims=True)
    unit = lax.rsqrt(total * (1.0 / 8192.0) + epsilon)
    for n in range(64):
        cols = slice(n * 128, (n + 1) * 128)
        v = x_ref[:, cols].astype(F32)
        nx[:, cols] = (v * unit * ag_ref[n : n + 1, :].astype(F32)).astype(BF16)

    pl.semaphore_wait(barrier, 38)

    def send_rows(k, carry):
        i = lax.rem(j + k, 32)
        send(
            nx.at[:, rows(i * 256, 256)],
            xn.at[rows(j * 16, 16), :],
            bsem.at[0],
            asem.at[0],
            (lax.div(i, 16), lax.rem(i, 16), z),
        )
        return carry

    lax.fori_loop(1, 32, send_rows, 0)
    xn[rows(j * 16, 16), :] = nx[:, rows(j * 256, 256)]

    traj = traj_ref[...].astype(F32)
    traj_cols = [column(traj[g : g + 1, :]) for g in range(4)]
    sub = lax.broadcasted_iota(jnp.int32, (128, 128), 0)
    lane = lax.broadcasted_iota(jnp.int32, (128, 128), 1)
    for g in range(4):
        step_col = jnp.zeros((128, 1), F32)
        step_row = jnp.zeros((1, 128), F32)
        for e in range(g + 1):
            same = jnp.where(traj_cols[g] == traj[e : e + 1, :], 1.0, 0.0)
            if e == g:
                same = jnp.where(lane < sub, same, 0.0)
            step_col = step_col + jnp.sum(same, axis=1, keepdims=True)
            same = jnp.where(traj_cols[e] == traj[g : g + 1, :], 1.0, 0.0)
            if e == g:
                same = jnp.where(sub < lane, same, 0.0)
            step_row = step_row + jnp.sum(same, axis=0, keepdims=True)
        slot_col = traj_cols[g] * 128.0 + step_col
        slot_row = traj[g : g + 1, :] * 128.0 + step_row
        for e in range(4):
            place_t[g * 128 : (g + 1) * 128, e * 128 : (e + 1) * 128] = jnp.where(
                (lane + e * 128).astype(F32) == slot_col, 1.0, 0.0
            ).astype(BF16)
            place[e * 128 : (e + 1) * 128, g * 128 : (g + 1) * 128] = jnp.where(
                (sub + e * 128).astype(F32) == slot_row, 1.0, 0.0
            ).astype(BF16)

    copies[1].wait()
    key_place = j * 1024 + lax.broadcasted_iota(jnp.int32, (128, 1024), 1)
    first_row = lax.broadcasted_iota(jnp.int32, (128, 1024), 0) == 0

    def turn_keys(t):
        keys_t[t, 0:128, :] = keys[t].T
        past = jnp.logical_and(first_row, key_place >= clen_ref[t])
        keys_t[t, 128:256, :] = jnp.where(past, masked_low, 0.0).astype(BF16)
        values[t, :, 128:256] = jnp.ones((1024, 128), BF16)

    turn_keys(0)
    turn_keys(1)

    own_traj = lax.div(row0, 128)
    own_step = lax.rem(row0, 128)
    cached = clen_ref[0]
    for t in range(1, 4):
        cached = jnp.where(own_traj == t, clen_ref[t], cached)
    lane16 = lane[0:16]
    angles = (cached + own_step + sub[0:16]).astype(F32) * spread_ref[...]
    cosine = jnp.cos(angles)
    sine = jnp.sin(angles)
    sine = jnp.where(lane16 < 64, -sine, sine)

    copies[0].wait()
    wait(xn.at[0:496], asem.at[0])

    def project(half):
        at = rows(half * 256, 256)
        xs[at, :] = dot(place[at, :], xn[...]).astype(BF16)
        part[at, 0:1024] = dot(xs[at, :], wq[...])
        part[at, 1024:1152] = dot(xs[at, :], wkv_ref[:, 0, :])
        part[at, 1152:1280] = dot(xs[at, :], wkv_ref[:, 1, :])

    project(1 - c)
    for k in (1, 2, 3, 0):
        q = turn(b, k)
        send(part.at[rows((1 - c) * 256 + q * 64, 64), :], r1.at[rows(q * 64, 64), :], bsem.at[2], p1r.at[q], sib)
    project(c)

    quarter = lax.rem(j, 4)
    holds_raw = lax.div(j, 4) == z

    @pl.when(holds_raw)
    def _():
        def send_raw(k, carry):
            i = lax.rem(j + k, 32)
            send(
                x_ref.at[:, rows(i * 256, 256)],
                raw.at[rows(quarter * 16, 16), :],
                bsem.at[1],
                rawr.at[quarter],
                (lax.div(i, 16), lax.rem(i, 16), z),
            )
            return carry

        lax.fori_loop(1, 32, send_raw, 0)
        raw[rows(quarter * 16, 16), :] = x_ref[:, rows(j * 256, 256)]

    turn_keys(2)

    def pair_sum(q):
        wait(r1.at[rows(q * 64, 64), :], p1r.at[q])
        return part[rows(c * 256 + q * 64, 64), :] + r1[rows(q * 64, 64), :]

    for k in (1, 2, 3):
        q = turn(a, k)
        s2[q] = pair_sum(q).astype(BF16)
        send(s2.at[q], r2.at[a], bsem.at[3], p2r.at[a], peer(q, b))
    sum2[...] = pair_sum(a)
    turn_keys(3)
    acc[...] = jnp.zeros(acc.shape, F32)
    for k in (3, 2, 1):
        q = turn(a, k)
        wait(r2.at[q], p2r.at[q])
        sum2[...] += r2[q].astype(F32)
    for k in (1, 2, 3):
        q = turn(b, k)
        send(sum2.at[rows(q * 16, 16), :], r3.at[b], bsem.at[4], p3r.at[b], peer(a, q))
    r3[b] = sum2[rows(b * 16, 16), :]
    for k in (3, 2, 1):
        q = turn(b, k)
        wait(r3.at[q], p3r.at[q])
    sums = (r3[0] + r3[1]) + (r3[2] + r3[3])
    mine = rows(row0, 16)
    for h in range(9):
        v = sums[:, h * 128 : (h + 1) * 128]
        qkv[mine, h * 128 : (h + 1) * 128] = (v * cosine + pltpu.roll(v, 64, 1) * sine).astype(BF16)
    qkv[mine, 1152:1280] = sums[:, 1152:1280].astype(BF16)

    a_up, a_down, a_far = turn(a, 1), turn(a, 3), turn(a, 2)
    b_up, b_down, b_far = turn(b, 1), turn(b, 3), turn(b, 2)

    def chunk(side, q):
        return rows(side * 256 + q * 64, 64)

    def half(q, n):
        return rows(c * 256 + q * 64 + n * 32, 32)

    def spread_start(ref, n, r_b, r_a, r_s):
        for k in (1, 2, 3):
            send(ref.at[mine, :], ref.at[mine, :], bsem.at[n], r_b.at[b], peer(a, turn(b, k)))
        for k in (3, 2, 1):
            q = turn(b, k)
            wait(ref.at[rows(c * 256 + a * 64 + q * 16, 16), :], r_b.at[q])
        at = ref.at[chunk(c, a), :]
        send(at, at, bsem.at[n + 1], r_a.at[a], peer(a_up, b))
        send(at, at, bsem.at[n + 1], r_a.at[a], peer(a_down, b))
        send(at, at, bsem.at[n + 2], r_s.at[a], sib)

    def spread_near(ref, n, r_a, r_s):
        for q, to, part_of, sem in ((a_down, a_up, 0, 0), (a_up, a_down, 1, 4)):
            at = ref.at[chunk(c, q), :]
            wait(at, r_a.at[q])
            at_half = ref.at[half(q, part_of), :]
            send(at_half, at_half, bsem.at[n + 1], r_a.at[q + sem], peer(to, b))
            send(at, at, bsem.at[n + 2], r_s.at[q], sib)

    def spread_far(ref, n, r_a, r_s):
        wait(ref.at[half(a_far, 0), :], r_a.at[a_far])
        wait(ref.at[half(a_far, 1), :], r_a.at[a_far + 4])
        at = ref.at[chunk(c, a_far), :]
        send(at, at, bsem.at[n + 2], r_s.at[a_far], sib)

    spread_start(qkv, 5, g1r, g2r, g3r)

    copies[2].wait()
    one = jnp.where(lax.broadcasted_iota(jnp.int32, (512, 128), 1) == 0, 1.0, 0.0).astype(BF16)
    lane64 = lane[0:64]

    def attend(side, q):
        at = chunk(side, q)
        t = side * 2 + lax.div(q, 2)
        heads = jnp.concatenate([qkv[at, h * 128 : (h + 1) * 128] for h in range(8)], axis=0)
        scores = dot(jnp.concatenate([heads, one], axis=1), keys_t[t])
        peak = jnp.max(scores, axis=1, keepdims=True)
        weights = jnp.exp2((scores - peak) * SCALE2).astype(BF16)
        out = dot(weights, values[t])
        peaks = jnp.zeros((64, 128), F32)
        masses = jnp.zeros((64, 128), F32)
        for h in range(8):
            head = slice(h * 64, (h + 1) * 64)
            o_all[at, h * 128 : (h + 1) * 128] = out[head, 0:128]
            peaks = jnp.where(lane64 == h, peak[head], peaks)
            masses = jnp.where(lane64 == h, out[head, 128:256], masses)
        ml_all[0, at, :] = peaks
        ml_all[1, at, :] = masses

    def attend_mine(n, carry):
        @pl.when(n == 1)
        def _():
            spread_near(qkv, 5, g2r, g3r)

        @pl.when(n == 2)
        def _():
            spread_far(qkv, 5, g2r, g3r)

        attend(c, turn(a, n))
        return carry

    def attend_other(n, carry):
        q = turn(b, jnp.where(n < 3, 2 - n, 3))
        wait(qkv.at[chunk(1 - c, q), :], g3r.at[q])
        attend(1 - c, q)
        at, to = chunk(1 - c, q), rows(q * 64, 64)
        send(o_all.at[at, :], rc1.at[to, :], bsem.at[8], c1r.at[q], sib)
        send(ml_all.at[:, at, :], rm1.at[:, to, :], bsem.at[9], c1r.at[q + 4], sib)
        return carry

    def join_pair(q):
        at, to = chunk(c, q), rows(q * 64, 64)
        wait(rc1.at[to, :], c1r.at[q])
        wait(rm1.at[:, to, :], c1r.at[q + 4])
        return merge(
            [
                (lambda h: o_all[at, h * 128 : (h + 1) * 128], ml_all[0, at, :], ml_all[1, at, :]),
                (lambda h: rc1[to, h * 128 : (h + 1) * 128], rm1[0, to, :], rm1[1, to, :]),
            ]
        )

    def send_joined(q):
        outs, top, mass = join_pair(q)
        for h in range(8):
            sc2[q, :, h * 128 : (h + 1) * 128] = outs[h].astype(BF16)
        sm2[q, 0] = top
        sm2[q, 1] = mass
        send(sc2.at[q], rc2.at[a], bsem.at[10], c2r.at[a], peer(q, b))
        send(sm2.at[q], rm2.at[a], bsem.at[11], c2r.at[a + 4], peer(q, b))

    lax.fori_loop(0, 3, attend_mine, 0)
    lax.fori_loop(0, 4, attend_other, 0)
    send_joined(a_far)
    send_joined(a_up)
    attend(c, a_down)
    send_joined(a_down)
    outs, top, mass = join_pair(a)
    for h in range(8):
        oc2[:, h * 128 : (h + 1) * 128] = outs[h]
    mc2[0] = top
    mc2[1] = mass

    own_rows = rows(own_traj * 128, 128)
    own_q = jnp.concatenate([qkv[mine, h * 128 : (h + 1) * 128] for h in range(8)], axis=0)
    own_scores = dot_nt(own_q, qkv[own_rows, 1024:1152])
    own_scores = jnp.where(lane <= own_step + (sub & 15), own_scores, masked_low)
    own_peak = jnp.max(own_scores, axis=1, keepdims=True)
    own_weights = jnp.exp2((own_scores - own_peak) * SCALE2)
    own_mass = jnp.sum(own_weights, axis=1, keepdims=True)
    own_out = dot(own_weights.astype(BF16), qkv[own_rows, 1152:1280])
    own_peaks = jnp.zeros((16, 128), F32)
    own_masses = jnp.zeros((16, 128), F32)
    for h in range(8):
        own_peaks = jnp.where(lane16 == h, own_peak[h * 16 : (h + 1) * 16], own_peaks)
        own_masses = jnp.where(lane16 == h, own_mass[h * 16 : (h + 1) * 16], own_masses)

    def arrived(k):
        q = turn(a, k)
        wait(rc2.at[q], c2r.at[q])
        wait(rm2.at[q], c2r.at[q + 4])
        return (lambda h: rc2[q, :, h * 128 : (h + 1) * 128].astype(F32), rm2[q, 0], rm2[q, 1])

    parts = [(lambda h: oc2[:, h * 128 : (h + 1) * 128], mc2[0], mc2[1])]
    parts += [arrived(k) for k in (2, 3, 1)]
    outs, top, mass = merge(parts)
    for h in range(8):
        oc2[:, h * 128 : (h + 1) * 128] = outs[h]
    mc2[0] = top
    mc2[1] = mass
    for k in (1, 2, 3):
        q = turn(b, k)
        send(oc2.at[rows(q * 16, 16), :], rc3.at[b], bsem.at[12], c3r.at[b], peer(a, q))
        send(mc2.at[:, rows(q * 16, 16), :], rm3.at[b], bsem.at[13], c3r.at[b + 4], peer(a, q))
    rc3[b] = oc2[rows(b * 16, 16), :]
    rm3[b] = mc2[:, rows(b * 16, 16), :]
    for k in (3, 2, 1):
        q = turn(b, k)
        wait(rc3.at[q], c3r.at[q])
        wait(rm3.at[q], c3r.at[q + 4])
    parts = [(lambda h, q=q: rc3[q, :, h * 128 : (h + 1) * 128], rm3[q, 0], rm3[q, 1]) for q in range(4)]
    parts.append((lambda h: own_out[h * 16 : (h + 1) * 16], own_peaks, own_masses))
    outs, top, mass = merge(parts)
    for h in range(8):
        ho[mine, h * 128 : (h + 1) * 128] = (outs[h] / mass[:, h : h + 1]).astype(BF16)

    spread_start(ho, 14, h1r, h2r, h3r)
    copies[3].wait()
    spread_near(ho, 14, h2r, h3r)
    spread_far(ho, 14, h2r, h3r)

    own_half = rows(c * 256, 256)
    hpb[own_half, :] = dot(ho[own_half, :], wo[...]).astype(BF16)
    for k in (0, 3, 1, 2):
        q = turn(b, k)
        wait(ho.at[chunk(1 - c, q), :], h3r.at[q])
    other_half = rows((1 - c) * 256, 256)
    hpb[other_half, :] = dot(ho[other_half, :], wo[...]).astype(BF16)

    def send_z(k, carry):
        q = lax.rem(z + k, 8)
        zs[q] = dot(place_t[rows(q * 64, 64), :], hpb[...]).astype(BF16)
        send(zs.at[q], zr.at[z], bsem.at[17], zrr.at[z], (c, s, q))
        return carry

    lax.fori_loop(1, 8, send_z, 0)
    total = dot(place_t[rows(z * 64, 64), :], hpb[...])
    for m in range(4):

        @pl.when(z * 4 + m != j)
        def _():
            wait(raw.at[rows(m * 16, 16), :], rawr.at[m])

    total = total + raw[...].astype(F32)
    for k in range(1, 8):
        q = lax.rem(z + 8 - k, 8)
        wait(zr.at[q], zrr.at[q])
        total = total + zr[q].astype(F32)
    attended = total.astype(BF16)
    att_ref[...] = attended
    attended = attended.astype(F32)
    my_z = rows(z * 64, 64)
    gains = fg_ref[...].astype(F32)
    gain_row = lax.broadcasted_iota(jnp.int32, (64, 128), 0)
    gain = [
        jnp.sum(jnp.where(gain_row == 2 * j + n, gains, 0.0), axis=0, keepdims=True) for n in (0, 1)
    ]
    gz[my_z, :] = (attended * jnp.concatenate(gain, axis=1)).astype(BF16)

    def send_feat_z(k, carry):
        ref = gz.at[my_z, :]
        send(ref, ref, bsem.at[18], zgr.at[z], (c, s, lax.rem(z + k, 8)))
        return carry

    lax.fori_loop(1, 8, send_feat_z, 0)

    squares = jnp.sum(attended * attended, axis=1, keepdims=True)
    squares = jnp.concatenate([jnp.broadcast_to(squares, (64, 128))] * 2, axis=0).T
    st[j] = squares[0:8]

    def send_squares(k, carry):
        i = lax.rem(j + k, 32)
        send(st.at[j], st.at[j], bsem.at[19], asem.at[1], (lax.div(i, 16), lax.rem(i, 16), z))
        return carry

    copies[4].wait()

    def multiply(*blocks):
        acc[...] += sum(dot(wv[:, rows(i * 256, 256)], feat[i]) for i in blocks)

    def send_block(i, dev):
        send(feat.at[i], feat.at[i], bsem.at[20], ftr.at[i], dev)

    def send_top(i, dev):
        send(feat.at[i, 0:128, :], feat.at[i, 0:128, :], bsem.at[20], ftr.at[i], dev)

    def send_bottom(i, dev):
        send(feat.at[i, 128:256, :], feat.at[i, 128:256, :], bsem.at[20], fbr.at[i], dev)

    def wait_halves(i):
        wait(feat.at[i, 0:128, :], ftr.at[i])
        wait(feat.at[i, 128:256, :], fbr.at[i])

    def fan(i):
        send_block(i, peer(a_up, b))
        send_block(i, peer(a_down, b))
        send_block(i, sib)

    def pass_chunk(k, carry):
        g = lax.rem(lax.div(z, 2) + jnp.where(k < 2, k, 5 - k), 4)
        for q in (2 * g, 2 * g + 1):

            @pl.when(q != z)
            def _():
                wait(gz.at[rows(q * 64, 64), :], zgr.at[q])

        at = rows(g * 128, 128)
        feat[j, :, at] = gz[at, :].T
        chunk = feat.at[j, :, at]
        for dev in (peer(a_up, b), peer(a_down, b), peer(a, b_up), peer(a, b_down), sib):
            send(chunk, chunk, bsem.at[20], ftr.at[j], dev)
        return carry

    lax.fori_loop(0, 4, pass_chunk, 0)
    i = blk(a, b_down)
    wait(feat.at[i], ftr.at[i])
    send_top(i, peer(a, b_up))
    fan(i)
    i = blk(a, b_up)
    wait(feat.at[i], ftr.at[i])
    send_bottom(i, peer(a, b_down))
    fan(i)

    for k in (8, 16, 24):
        send_squares(k, 0)
    i = blk(a, b_far)
    wait_halves(i)
    fan(i)

    def b_order(b_, n):
        step = jnp.where(n == 0, 0, jnp.where(n == 1, 3, n - 1))
        return lax.rem(b_ + step, 4)

    def sib_blk(a_, b_):
        return (1 - c) * 16 + seq_of(1 - c, a_, b_)

    def ready(i):
        wait(feat.at[i], ftr.at[i])
        return i

    def near(n, carry):
        bn = b_order(b, n)
        i = ready(blk(a_down, bn))
        send_top(i, peer(a_up, b))
        send_block(i, sib)
        k = ready(blk(a_up, bn))
        send_bottom(k, peer(a_down, b))
        send_block(k, sib)
        lax.fori_loop(8 * n + 1, 8 * n + 8, send_squares, 0)
        multiply(blk(a, bn), i, k, ready(sib_blk(b, b_order(a, n))))
        return carry

    lax.fori_loop(0, 4, near, 0)

    wait(st.at[0:31], asem.at[1])
    sum_sq = st[0]
    for n in range(1, 32):
        sum_sq = sum_sq + st[n]
    zt[z] = sum_sq

    def send_sum_sq(k, carry):
        send(zt.at[z], zt.at[z], bsem.at[21], ztr.at[z], (c, s, lax.rem(z + k, 8)))
        return carry

    lax.fori_loop(1, 8, send_sum_sq, 0)

    def far(n, carry):
        i = blk(a_far, b_order(b, n))
        wait_halves(i)
        send_block(i, sib)
        sn = b_order(a, n)
        multiply(i, ready(sib_blk(turn(b, 3), sn)), ready(sib_blk(turn(b, 1), sn)))
        return carry

    lax.fori_loop(0, 4, far, 0)

    def last(n, carry):
        multiply(*[ready(sib_blk(turn(b, 2), b_order(a, 2 * n + e))) for e in (0, 1)])
        return carry

    lax.fori_loop(0, 2, last, 0)

    for k in range(1, 8):
        q = lax.rem(z + 8 - k, 8)
        wait(zt.at[q], ztr.at[q])
    entries = acc.shape[0]
    offset = (j * 8 + z) * entries
    entry = offset + lax.broadcasted_iota(jnp.int32, (entries, 128), 0)
    for g in range(4):
        sum_sq = jnp.where(lane[0:1] < 64, zt[2 * g][0:1], zt[2 * g + 1][0:1])
        logits = acc[:, g * 128 : (g + 1) * 128] * lax.rsqrt(sum_sq * (1.0 / 8192.0) + epsilon)
        peak = jnp.max(logits, axis=0, keepdims=True)
        fs[c, g : g + 1, :] = peak
        fs[c, 4 + g : 5 + g, :] = jnp.sum(jnp.exp(logits - peak), axis=0, keepdims=True)
        fs[c, 8 + g : 9 + g, :] = jnp.sum(
            jnp.where(entry == tok_ref[g : g + 1, :], logits, 0.0), axis=0, keepdims=True
        )
    fs[c, 12:16, :] = jnp.zeros((4, 128), F32)

    def join_stats(stage, place_in, peers):
        count = len(peers) + 1
        base = stage * 8
        for dev in peers:
            ref = fs.at[base + place_in]
            send(ref, ref, bsem.at[22], fsr.at[base + place_in], dev)
        for k in range(1, count):
            at = base + lax.rem(place_in + k, count)
            wait(fs.at[at], fsr.at[at])
        top = fs[base, 0:4, :]
        for n in range(1, count):
            top = jnp.maximum(top, fs[base + n, 0:4, :])
        exp_total = jnp.zeros((4, 128), F32)
        picked_total = jnp.zeros((4, 128), F32)
        for n in range(count):
            exp_total = exp_total + fs[base + n, 4:8, :] * jnp.exp(fs[base + n, 0:4, :] - top)
            picked_total = picked_total + fs[base + n, 8:12, :]
        return top, exp_total, picked_total

    def keep_stats(at, stats):
        for n in range(3):
            fs[at, n * 4 : n * 4 + 4, :] = stats[n]
        fs[at, 12:16, :] = jnp.zeros((4, 128), F32)

    keep_stats(8 + along, join_stats(0, c, [sib]))
    keep_stats(16 + across, join_stats(1, along, [(c, turn(along, k) * 4 + across, z) for k in (1, 2, 3)]))
    keep_stats(24 + z, join_stats(2, across, [(c, along * 4 + turn(across, k), z) for k in (1, 2, 3)]))
    top, exp_total, picked_total = join_stats(3, z, [(c, s, lax.rem(z + k, 8)) for k in (4, 3, 5, 2, 6, 1, 7)])
    lp_ref[...] = picked_total - top - jnp.log(exp_total)

    wait(xn.at[0:496], bsem.at[0])

    @pl.when(holds_raw)
    def _():
        wait(xn.at[0:496], bsem.at[1])

    wait(r1, bsem.at[2])
    wait(r2.at[0:3], bsem.at[3])
    wait(r3.at[0:3], bsem.at[4])
    for ref, n in ((qkv, 5), (ho, 14)):
        wait(ref.at[0:48], bsem.at[n])
        wait(ref.at[0:192], bsem.at[n + 1])
        wait(ref.at[0:256], bsem.at[n + 2])
    wait(rc1, bsem.at[8])
    wait(rm1, bsem.at[9])
    wait(rc2.at[0:3], bsem.at[10])
    wait(rm2.at[0:3], bsem.at[11])
    wait(rc3.at[0:3], bsem.at[12])
    wait(rm3.at[0:3], bsem.at[13])
    wait(zr.at[0:7], bsem.at[17])
    wait(zr.at[0:7], bsem.at[18])
    wait(st.at[0:31], bsem.at[19])
    wait(feat.at[0:31], bsem.at[20])
    wait(zt.at[0:7], bsem.at[21])
    wait(fs.at[0:14], bsem.at[22])


def per_device(
    x_rows,
    attn_gain,
    final_gain,
    w_query,
    w_kv,
    w_out,
    kv_cache,
    w_vocab,
    token_ids,
    cache_len,
    row_traj,
):
    entries = w_vocab.shape[1]
    spread = np.exp(np.arange(HD // 2) * (-2.0 * math.log(rope_base) / HD)).astype(np.float32)
    vmem = pl.BlockSpec(memory_space=pltpu.VMEM)
    smem = pl.BlockSpec(memory_space=pltpu.SMEM)
    hbm = pl.BlockSpec(memory_space=pl.ANY)
    dma = pltpu.SemaphoreType.DMA
    attended, logprob = pl.pallas_call(
        kernel,
        out_shape=(
            jax.ShapeDtypeStruct((64, 256), BF16),
            jax.ShapeDtypeStruct((4, 128), F32),
        ),
        in_specs=[vmem, vmem, vmem, hbm, vmem, hbm, hbm, hbm, vmem, smem, vmem, vmem],
        out_specs=(vmem, vmem),
        scratch_shapes=[
            pltpu.VMEM((256, 1024), BF16),
            pltpu.VMEM((1024, 256), BF16),
            pltpu.VMEM((4, 1024, 128), BF16),
            pltpu.VMEM((4, 256, 1024), BF16),
            pltpu.VMEM((4, 1024, 256), BF16),
            pltpu.VMEM((entries, 8192), BF16),
            pltpu.VMEM((16, 8192), BF16),
            pltpu.VMEM((512, 256), BF16),
            pltpu.VMEM((64, 256), BF16),
            pltpu.VMEM((512, 512), BF16),
            pltpu.VMEM((512, 512), BF16),
            pltpu.VMEM((512, 256), BF16),
            pltpu.VMEM((512, 1280), F32),
            pltpu.VMEM((256, 1280), F32),
            pltpu.VMEM((4, 64, 1280), BF16),
            pltpu.VMEM((4, 64, 1280), BF16),
            pltpu.VMEM((64, 1280), F32),
            pltpu.VMEM((4, 16, 1280), F32),
            pltpu.VMEM((512, 1280), BF16),
            pltpu.VMEM((512, 1024), F32),
            pltpu.VMEM((2, 512, 128), F32),
            pltpu.VMEM((256, 1024), F32),
            pltpu.VMEM((2, 256, 128), F32),
            pltpu.VMEM((4, 64, 1024), BF16),
            pltpu.VMEM((4, 2, 64, 128), F32),
            pltpu.VMEM((4, 64, 1024), BF16),
            pltpu.VMEM((4, 2, 64, 128), F32),
            pltpu.VMEM((64, 1024), F32),
            pltpu.VMEM((2, 64, 128), F32),
            pltpu.VMEM((4, 16, 1024), F32),
            pltpu.VMEM((4, 2, 16, 128), F32),
            pltpu.VMEM((512, 1024), BF16),
            pltpu.VMEM((512, 256), BF16),
            pltpu.VMEM((8, 64, 256), BF16),
            pltpu.VMEM((8, 64, 256), BF16),
            pltpu.VMEM((512, 256), BF16),
            pltpu.VMEM((32, 256, 512), BF16),
            pltpu.VMEM((entries, 512), F32),
            pltpu.VMEM((32, 8, 128), F32),
            pltpu.VMEM((8, 8, 128), F32),
            pltpu.VMEM((32, 16, 128), F32),
            dma((5,)),
            dma((23,)),
            dma((2,)),
            dma((4,)),
            dma((4,)),
            dma((4,)),
            dma((4,)),
            dma((4,)),
            dma((8,)),
            dma((4,)),
            dma((8,)),
            dma((8,)),
            dma((8,)),
            dma((4,)),
            dma((8,)),
            dma((4,)),
            dma((8,)),
            dma((8,)),
            dma((32,)),
            dma((32,)),
            dma((8,)),
            dma((32,)),
        ],
        compiler_params=pltpu.CompilerParams(
            collective_id=0, has_side_effects=True, vmem_limit_bytes=60 * 1024 * 1024
        ),
        cost_estimate=pl.CostEstimate(
            flops=8_000_000_000, bytes_accessed=14_000_000, transcendentals=5_000_000
        ),
    )(
        x_rows,
        attn_gain.reshape(64, 128),
        final_gain.reshape(64, 128),
        w_query,
        w_kv,
        w_out,
        kv_cache,
        w_vocab.T,
        token_ids.reshape(4, 128),
        cache_len,
        row_traj.reshape(4, 128),
        jnp.asarray(np.concatenate([spread, spread])[None]),
    )
    return attended, logprob.reshape(-1)


def solution(mesh):
    in_specs = (
        P(("side", "seq"), None),
        P(),
        P(),
        P(("side", "seq"), "tensor"),
        P(("side", "seq"), None, "tensor"),
        P("tensor", ("side", "seq")),
        P(None, None, ("side", "seq"), "tensor"),
        P(None, ("side", "seq", "tensor")),
        P(),
        P(),
        P(),
    )
    out_specs = (P("tensor", ("side", "seq")), P())
    return jax.shard_map(
        per_device, mesh=mesh, in_specs=in_specs, out_specs=out_specs, check_vma=False
    )
```

time: 167 us -> 145 us (0.87)
  local copies, waits for them, and re-layouts: 21 us -> 2.62 us
  other arithmetic: 2.11 us -> 0 us
    unnamed x4 -> x2, local copies, waits for them, and re-layouts: 18.3 us -> 2.62 us
    reshape x2 -> x0, local copies, waits for them, and re-layouts: 2.7 us -> none  [the longest x1 1.35 us: per_device(): final_gain.reshape(1, -1)]
where the time goes in v3:
time: 145 us; the launch traced here: 144 us
  Pallas kernels  141 us (97%)
  local copies, waits for them, and re-layouts  2.62 us (2%)
    pallas_call x1, Pallas kernels, per_device(): pl.pallas_call(kernel, out_shape=(jax.ShapeDtypeStruct((64, 256), BF16),...  141 us

profile of v3, /device:TPU:32, one launch (start us, length us, event | category | flops | bytes accessed | tf_op | source)
XLA Modules:
  0.0 144.5 jit_solution(7222383692127064166)
XLA Ops:
  0.6 141.2 %shard_map.131 = (bf16[64,256]{1,0:T(8,128)(2,1)}, f32[4,128]{1,0:T(4,128)}) custom-call(bf16[16,8192]{1,0:T(8,128)(2,1)} %x_ref.1, bf16[64,128]{1,0:T(8,128)(2,1)} %bitcast.8, bf16[64,128]{1,0:T(8,128)(2,1)} %bitcast.9, bf16[256,1024]{1,0:T(8,128)(2,1)} %wq_hbm.1, bf16[256,2,128]{2,1,0:T(2,128)(2,1)} %wkv_ref.1, bf16[1024,256]{1,0:T(8,128)(2,1)} %wo_hbm.1, ...), custom_call_target="tpu_custom_call" | custom-call | flops 8000000000 | bytes 14000000 | tf_op jit(solution)/shard_map/pallas_call | solution.py:746
  141.8 1.4 copy.16
  143.2 1.2 copy.17

commit v4 on v0

v4 whole, which is shorter than its diff:
```python
import functools
import math

import jax
import jax.numpy as jnp
import numpy as np
from jax import lax
from jax.experimental import pallas as pl
from jax.experimental.pallas import tpu as pltpu
from jax.sharding import PartitionSpec as P

HD = 128
TRAJ = 4
MESH = pl.DeviceIdType.MESH

epsilon = 1e-06
rope_base = 1000000.0
masked_low = -1e30
SCALE2 = float(HD) ** (-0.5) * math.log2(math.e)

F32 = jnp.float32
BF16 = jnp.bfloat16


def dot(a, b):
    return jnp.dot(a, b, preferred_element_type=F32)


def dot_nt(a, b):
    return lax.dot_general(a, b, (((1,), (1,)), ((), ())), preferred_element_type=F32)


def rows(start, size):
    return pl.ds(pl.multiple_of(start, size), size)


def column(row):
    return jnp.broadcast_to(row, (128, 128)).T


def merge(parts):
    top = functools.reduce(jnp.maximum, [p[1] for p in parts])
    factors = [jnp.exp2((p[1] - top) * SCALE2) for p in parts]
    mass = sum(pltpu.roll(p[1], 120, 1) * f for p, f in zip(parts, factors))
    outs = [
        sum(p[0](h) * f[:, h : h + 1] for p, f in zip(parts, factors)) for h in range(8)
    ]
    return outs, top, mass


def pack(top, mass):
    lane = lax.broadcasted_iota(jnp.int32, top.shape, 1)
    return jnp.where(lane < 8, top, jnp.where(lane < 16, pltpu.roll(mass, 8, 1), 0.0))


def encode(stats):
    lane = lax.broadcasted_iota(jnp.int32, stats.shape, 1)
    high = stats.astype(BF16).astype(F32)
    middle = (stats - high).astype(BF16).astype(F32)
    low = (stats - high) - middle
    terms = jnp.where(lane < 32, pltpu.roll(middle, 16, 1), pltpu.roll(low, 32, 1))
    return jnp.where(lane < 16, high, jnp.where(lane < 48, terms, 0.0)).astype(BF16)


def decode(terms):
    terms = terms.astype(F32)
    return (terms + pltpu.roll(terms, 112, 1)) + pltpu.roll(terms, 96, 1)


def kernel(
    x_ref,
    ag_ref,
    fg_ref,
    wq_hbm,
    wkv_ref,
    wo_hbm,
    kv_hbm,
    wv_hbm,
    tok_ref,
    clen_ref,
    traj_ref,
    spread_ref,
    att_ref,
    lp_ref,
    wq,
    wo,
    keys,
    keys_t,
    values,
    wv,
    wv_sib,
    nx,
    xn,
    raw,
    raw_s,
    place,
    place_t,
    toks,
    trig,
    xs,
    part,
    r1,
    s2,
    r2,
    x3,
    r3,
    qkv,
    o_all,
    rc1,
    sc2,
    rc2,
    oc2,
    mc2,
    rc3,
    ho,
    hp,
    hpb,
    zr,
    attz,
    feat,
    acc,
    racc,
    st,
    fs,
    fz,
    lsem,
    bsem,
    asem,
    p1r,
    p2r,
    p3r,
    g2r,
    g3r,
    c1r,
    c2r,
    c3r,
    h2r,
    h3r,
    zrr,
    zgr,
    ftr,
    fbr,
    wvr,
    rar,
):
    c = lax.axis_index("side")
    s = lax.axis_index("seq")
    z = lax.axis_index("tensor")
    j = c * 16 + s
    along = lax.div(s, 4)
    across = lax.rem(s, 4)
    a = along + c * (across - along)
    b = across + c * (along - across)

    def seq_of(side, a_, b_):
        straight = a_ * 4 + b_
        return straight + side * (b_ * 4 + a_ - straight)

    def blk(a_, b_):
        return seq_of(c, a_, b_)

    def peer(a_, b_):
        return (c, seq_of(c, a_, b_), z)

    def turn(v, k):
        return lax.rem(v + k, 4)

    sib = (1 - c, s, z)

    def plane(k):
        i = lax.rem(j + k, 32)
        return i, (lax.div(i, 16), lax.rem(i, 16), z)

    def column_of(k):
        q = lax.rem(z + k, 8)
        return q, (c, s, q)

    def send(src, dst, ssem, rsem, dev):
        pltpu.make_async_remote_copy(
            src_ref=src, dst_ref=dst, send_sem=ssem, recv_sem=rsem, device_id=dev, device_id_type=MESH
        ).start()

    def wait(ref, sem):
        pltpu.make_async_copy(ref, ref, sem).wait()

    def local(src, dst, n):
        return pltpu.make_async_copy(src, dst, lsem.at[n])

    def each(low, high, body):
        def step(k, carry):
            body(k)
            return carry

        lax.fori_loop(low, high, step, 0)

    copies = [
        local(wq_hbm, wq, 0),
        local(kv_hbm.at[0], keys, 1),
        local(kv_hbm.at[1], values.at[:, :, 0:128], 2),
        local(wo_hbm, wo, 3),
        local(wv_hbm.at[:, rows(c * 4096, 4096)], wv, 4),
    ]
    for copy in copies:
        copy.start()

    barrier = pltpu.get_barrier_semaphore()

    def greet(k):
        pl.semaphore_signal(barrier, inc=1, device_id=plane(k)[1], device_id_type=MESH)

    def greet_z(k):
        pl.semaphore_signal(barrier, inc=1, device_id=column_of(k)[1], device_id_type=MESH)

    each(1, 32, greet)
    each(1, 8, greet_z)

    def greet_sib_z(k):
        q, _ = column_of(k)
        pl.semaphore_signal(barrier, inc=1, device_id=(1 - c, s, q), device_id_type=MESH)

    each(1, 8, greet_sib_z)

    total = jnp.zeros((16, 1), F32)
    for n in range(8):
        v = x_ref[:, n * 1024 : (n + 1) * 1024].astype(F32)
        total = total + jnp.sum(v * v, axis=1, keepdims=True)
    unit = lax.rsqrt(total * (1.0 / 8192.0) + epsilon)
    for n in range(64):
        cols = slice(n * 128, (n + 1) * 128)
        v = x_ref[:, cols].astype(F32)
        nx[:, cols] = (v * unit * ag_ref[n : n + 1, :].astype(F32)).astype(BF16)

    pl.semaphore_wait(barrier, 45)

    def send_weights(n):
        send(
            wv_hbm.at[:, rows((1 - c) * 4096 + n * 1024, 1024)],
            wv_sib.at[:, n * 1024 : (n + 1) * 1024],
            bsem.at[28],
            wvr.at[n],
            sib,
        )

    here = rows(j * 16, 16)

    def send_rows(k):
        i, dev = plane(k)
        send(nx.at[:, rows(i * 256, 256)], xn.at[here, :], bsem.at[0], asem.at[0], dev)

    def send_raw(k):
        i, dev = plane(k)
        send(x_ref.at[:, rows(i * 256, 256)], raw.at[here, :], bsem.at[1], asem.at[1], dev)

    each(1, 32, send_rows)
    xn[here, :] = nx[:, rows(j * 256, 256)]
    raw[here, :] = x_ref[:, rows(j * 256, 256)]

    traj = traj_ref[...].astype(F32)
    traj_cols = [column(traj[g : g + 1, :]) for g in range(4)]
    sub = lax.broadcasted_iota(jnp.int32, (128, 128), 0)
    lane = lax.broadcasted_iota(jnp.int32, (128, 128), 1)
    for g in range(4):
        step_col = jnp.zeros((128, 1), F32)
        step_row = jnp.zeros((1, 128), F32)
        for e in range(g + 1):
            same = jnp.where(traj_cols[g] == traj[e : e + 1, :], 1.0, 0.0)
            if e == g:
                same = jnp.where(lane < sub, same, 0.0)
            step_col = step_col + jnp.sum(same, axis=1, keepdims=True)
            same = jnp.where(traj_cols[e] == traj[g : g + 1, :], 1.0, 0.0)
            if e == g:
                same = jnp.where(sub < lane, same, 0.0)
            step_row = step_row + jnp.sum(same, axis=0, keepdims=True)
        slot_col = traj_cols[g] * 128.0 + step_col
        slot_row = traj[g : g + 1, :] * 128.0 + step_row
        for e in range(4):
            place_t[g * 128 : (g + 1) * 128, e * 128 : (e + 1) * 128] = jnp.where(
                (lane + e * 128).astype(F32) == slot_col, 1.0, 0.0
            ).astype(BF16)
            place[e * 128 : (e + 1) * 128, g * 128 : (g + 1) * 128] = jnp.where(
                (sub + e * 128).astype(F32) == slot_row, 1.0, 0.0
            ).astype(BF16)

    key_place = j * 1024 + lax.broadcasted_iota(jnp.int32, (128, 1024), 1)
    first_row = lax.broadcasted_iota(jnp.int32, (128, 1024), 0) == 0

    def turn_keys(t):
        keys_t[t, 0:128, :] = keys[t].T
        past = jnp.logical_and(first_row, key_place >= clen_ref[t])
        keys_t[t, 128:256, :] = jnp.where(past, masked_low, 0.0).astype(BF16)
        values[t, :, 128:256] = jnp.ones((1024, 128), BF16)

    copies[0].wait()
    wait(xn.at[0:496], asem.at[0])

    def project(half):
        at = rows(half * 256, 256)
        xs[at, :] = dot(place[at, :], xn[...]).astype(BF16)
        part[at, 0:1024] = dot(xs[at, :], wq[...])
        part[at, 1024:1152] = dot(xs[at, :], wkv_ref[:, 0, :])
        part[at, 1152:1280] = dot(xs[at, :], wkv_ref[:, 1, :])

    def group(side, p):
        return rows((side * 2 + p // 2) * 128 + (p % 2) * 64, 64)

    def slab(p, q):
        return rows((c * 2 + p // 2) * 128 + (p % 2) * 64 + q * 16, 16)

    project(1 - c)
    for p in range(4):
        send(part.at[group(1 - c, p), :], r1.at[p], bsem.at[4 + p], p1r.at[p], sib)
    each(1, 16, send_raw)
    project(c)
    each(16, 32, send_raw)

    def reduce_a(p):
        wait(r1.at[p], p1r.at[p])
        for k in (2, 1, 3):
            q = turn(a, k)
            s2[p, q] = (part[slab(p, q), :] + r1[p, rows(q * 16, 16), :]).astype(BF16)
            send(s2.at[p, q], r2.at[p, a], bsem.at[8 + p], p2r.at[p * 4 + a], peer(q, b))
        x3[p] = part[slab(p, a), :] + r1[p, rows(a * 16, 16), :]

    def reduce_b(p):
        for k in (1, 3, 2):
            q = turn(a, k)
            wait(r2.at[p, q], p2r.at[p * 4 + q])
            x3[p] += r2[p, q].astype(F32)
        for k in (2, 1, 3):
            send(x3.at[p], r3.at[p, b], bsem.at[12 + p], p3r.at[p * 4 + b], peer(a, turn(b, k)))
        r3[p, b] = x3[p]

    def rotate(p):
        for k in (1, 3, 2):
            q = turn(b, k)
            wait(r3.at[p, q], p3r.at[p * 4 + q])
        at = slab(p, a)
        cosine, sine = trig[p, 0], trig[p, 1]
        for h in range(10):
            cols = slice(h * 128, (h + 1) * 128)
            v = (r3[p, 0, :, cols] + r3[p, 1, :, cols]) + (r3[p, 2, :, cols] + r3[p, 3, :, cols])
            if h < 9:
                v = v * cosine + pltpu.roll(v, 64, 1) * sine
            qkv[at, cols] = v.astype(BF16)

    def gather_a(p, ref, n, sems):
        ref = ref.at[slab(p, a), :]
        for k in (2, 1, 3):
            send(ref, ref, bsem.at[2 * n + p], sems.at[p * 4 + a], peer(turn(a, k), b))

    def gather_sib(p, ref, n, sems, to):
        for k in (1, 3, 2):
            q = turn(a, k)
            wait(ref.at[slab(p, q), :], sems.at[p * 4 + q])
        ref = ref.at[group(c, p), :]
        send(ref, ref, bsem.at[2 * n + p], to.at[p], sib)

    lane16 = lane[0:16]

    def angles():
        for p in range(4):
            cached = jnp.where(c == 0, clen_ref[p // 2], clen_ref[2 + p // 2])
            turned = (cached + (p % 2) * 64 + a * 16 + sub[0:16]).astype(F32) * spread_ref[...]
            trig[p, 0] = jnp.cos(turned)
            sine = jnp.sin(turned)
            trig[p, 1] = jnp.where(lane16 < 64, -sine, sine)

    def z_rows(p, q):
        return rows((lax.div(q, 4) * 2 + p // 2) * 128 + (p % 2) * 64 + lax.rem(q, 4) * 16, 16)


    def group_raw():
        wait(raw.at[0:496], asem.at[1])
        for p in range(4):
            raw_s[p] = dot(place[z_rows(p, z), :], raw[...])

    def group_tokens():
        token = tok_ref[...].astype(F32)
        token_cols = [column(token[g : g + 1, :]) for g in range(4)]
        grouped = [
            sum(
                jnp.sum(
                    place_t[g * 128 : (g + 1) * 128, t * 128 : (t + 1) * 128].astype(F32) * token_cols[g],
                    axis=0,
                    keepdims=True,
                )
                for g in range(4)
            )
            for t in range(4)
        ]
        for p in range(4):
            first, second = grouped[p // 2], grouped[2 + p // 2]
            if p % 2 == 0:
                toks[p : p + 1, :] = jnp.where(lane[0:1] < 64, first, pltpu.roll(second, 64, 1))
            else:
                toks[p : p + 1, :] = jnp.where(lane[0:1] < 64, pltpu.roll(first, 64, 1), second)
        acc[...] = jnp.zeros(acc.shape, F32)

    one = jnp.where(lax.broadcasted_iota(jnp.int32, (256, 128), 1) == 0, 1.0, 0.0).astype(BF16)
    lane64 = lane[0:64]

    def attend(side, p):
        at = group(side, p)
        t = side * 2 + p // 2
        stats = jnp.zeros((64, 128), F32)
        for h in range(0, 8, 4):
            heads = jnp.concatenate(
                [qkv[at, (h + e) * 128 : (h + e + 1) * 128] for e in range(4)], axis=0
            )
            scores = dot(jnp.concatenate([heads, one], axis=1), keys_t[t])
            peak = jnp.max(scores, axis=1, keepdims=True)
            weights = jnp.exp2((scores - peak) * SCALE2).astype(BF16)
            out = dot(weights, values[t])
            for e in range(4):
                head = slice(e * 64, (e + 1) * 64)
                o_all[at, (h + e) * 128 : (h + e + 1) * 128] = out[head, 0:128]
                stats = jnp.where(lane64 == h + e, peak[head], stats)
                stats = jnp.where(lane64 == 8 + h + e, out[head, 128:256], stats)
        o_all[at, 1024:1152] = stats

    def attend_sib(p):
        at = group(1 - c, p)
        wait(qkv.at[at, :], g3r.at[p])
        attend(1 - c, p)
        send(o_all.at[at, :], rc1.at[p], bsem.at[24 + p], c1r.at[p], sib)

    def join_a(p):
        wait(rc1.at[p], c1r.at[p])

        def joined(q):
            at, to = slab(p, q), rows(q * 16, 16)
            return merge(
                [
                    (lambda h: o_all[at, h * 128 : (h + 1) * 128], o_all[at, 1024:1152]),
                    (lambda h: rc1[p, to, h * 128 : (h + 1) * 128], rc1[p, to, 1024:1152]),
                ]
            )

        for k in (2, 1, 3):
            q = turn(a, k)
            outs, top, mass = joined(q)
            for h in range(8):
                sc2[p, q, :, h * 128 : (h + 1) * 128] = outs[h].astype(BF16)
            sc2[p, q, :, 1024:1152] = encode(pack(top, mass))
            send(sc2.at[p, q], rc2.at[p, a], bsem.at[32 + p], c2r.at[p * 4 + a], peer(q, b))
        outs, top, mass = joined(a)
        for h in range(8):
            oc2[p, :, h * 128 : (h + 1) * 128] = outs[h]
        mc2[p] = pack(top, mass)

    def join_b(p):
        def arrived(k):
            q = turn(a, k)
            wait(rc2.at[p, q], c2r.at[p * 4 + q])
            return (lambda h: rc2[p, q, :, h * 128 : (h + 1) * 128].astype(F32), decode(rc2[p, q, :, 1024:1152]))

        parts = [(lambda h: oc2[p, :, h * 128 : (h + 1) * 128], mc2[p])]
        parts += [arrived(k) for k in (1, 3, 2)]
        outs, top, mass = merge(parts)
        for h in range(8):
            rc3[p, b, :, h * 128 : (h + 1) * 128] = outs[h].astype(BF16)
        rc3[p, b, :, 1024:1152] = encode(pack(top, mass))
        for k in (2, 1, 3):
            dev = peer(a, turn(b, k))
            send(rc3.at[p, b], rc3.at[p, b], bsem.at[40 + p], c3r.at[p * 4 + b], dev)

    def join_own(p):
        at = slab(p, a)
        count = 64 * (1 + p % 2)
        keys_at = rows((c * 2 + p // 2) * 128, count)
        own_q = jnp.concatenate([qkv[at, h * 128 : (h + 1) * 128] for h in range(8)], axis=0)
        scores = dot_nt(own_q, qkv[keys_at, 1024:1152])
        step = lax.broadcasted_iota(jnp.int32, (128, count), 0) & 15
        key = lax.broadcasted_iota(jnp.int32, (128, count), 1)
        scores = jnp.where(key <= (p % 2) * 64 + a * 16 + step, scores, masked_low)
        peak = jnp.max(scores, axis=1, keepdims=True)
        weights = jnp.exp2((scores - peak) * SCALE2)
        mass = jnp.sum(weights, axis=1, keepdims=True)
        out = dot(weights.astype(BF16), qkv[keys_at, 1152:1280])
        stats = jnp.zeros((16, 128), F32)
        for h in range(8):
            head = slice(h * 16, (h + 1) * 16)
            stats = jnp.where(lane16 == h, peak[head], stats)
            stats = jnp.where(lane16 == 8 + h, mass[head], stats)
        for k in (1, 3, 2):
            q = turn(b, k)
            wait(rc3.at[p, q], c3r.at[p * 4 + q])
        parts = [
            (lambda h, q=q: rc3[p, q, :, h * 128 : (h + 1) * 128].astype(F32), decode(rc3[p, q, :, 1024:1152]))
            for q in range(4)
        ]
        parts.append((lambda h: out[h * 16 : (h + 1) * 16], stats))
        outs, top, mass = merge(parts)
        for h in range(8):
            ho[at, h * 128 : (h + 1) * 128] = (outs[h] / mass[:, h : h + 1]).astype(BF16)
        gather_a(p, ho, 24, h2r)

    def project_out(p):
        def half(side):
            at = group(side, p)
            hp[at, :] = dot(ho[at, :], wo[...])
            hpb[at, :] = hp[at, :].astype(BF16)

        half(c)
        wait(ho.at[group(1 - c, p), :], h3r.at[p])
        half(1 - c)

        def send_z(k):
            q, dev = column_of(lax.rem(4 + lax.div(k, 2) * (1 - 2 * lax.rem(k, 2)) + 8, 8))
            send(hpb.at[z_rows(p, q), :], zr.at[p, z], bsem.at[56 + p], zrr.at[p * 8 + z], dev)

        each(1, 8, send_z)

    def attended(p):
        my_z = z_rows(p, z)
        total = raw_s[p] + hp[my_z, :]
        for k in (1, 7, 2, 6, 3, 5, 4):
            q = lax.rem(z + k, 8)
            wait(zr.at[p, q], zrr.at[p * 8 + q])
            total = total + zr[p, q].astype(F32)
        attz[my_z, :] = total.astype(BF16)

        def send_z(k):
            q, dev = column_of(lax.rem(4 + lax.div(k, 2) * (1 - 2 * lax.rem(k, 2)) + 8, 8))
            ref = attz.at[my_z, :]
            send(ref, ref, bsem.at[60 + p], zgr.at[p * 8 + z], dev)

        each(1, 8, send_z)

    a_up, a_down, a_far = turn(a, 1), turn(a, 3), turn(a, 2)
    b_up, b_down, b_far = turn(b, 1), turn(b, 3), turn(b, 2)

    gains = fg_ref[...].astype(F32)
    gain_row = lax.broadcasted_iota(jnp.int32, (64, 128), 0)
    gain_col = jnp.concatenate(
        [
            column(jnp.sum(jnp.where(gain_row == 2 * j + n, gains, 0.0), axis=0, keepdims=True))
            for n in (0, 1)
        ],
        axis=0,
    )

    def features(p):
        for k in (1, 7, 2, 6, 3, 5, 4):
            q = lax.rem(z + k, 8)
            wait(attz.at[z_rows(p, q), :], zgr.at[p * 8 + q])
        turned = jnp.concatenate([attz[group(0, p), :], attz[group(1, p), :]], axis=0).T.astype(F32)
        st[j, p : p + 1, :] = jnp.sum(turned * turned, axis=0, keepdims=True)
        feat[p // 2, s, :, lanes(p)] = (turned * gain_col).astype(BF16)
        for dev in (peer(a_up, b), peer(a_down, b), peer(a, b_up), peer(a, b_down)):
            send_block(p, s, dev)

    def send_squares(k):
        send(st.at[j], st.at[j], bsem.at[68], asem.at[2], plane(k)[1])

    def multiply(pair, *blocks):
        acc[0, pair] += sum(dot(wv[:, rows(i * 256, 256)], feat[pair, i]) for i in blocks)
        acc[1, pair] += sum(dot(wv_sib[:, rows(i * 256, 256)], feat[pair, i]) for i in blocks)

    def lanes(p):
        return slice((p % 2) * 128, (p % 2) * 128 + 128)

    def block(p, i):
        return feat.at[p // 2, i, :, lanes(p)]

    def top(p, i):
        return feat.at[p // 2, i, 0:128, lanes(p)]

    def bottom(p, i):
        return feat.at[p // 2, i, 128:256, lanes(p)]

    def send_block(p, i, dev):
        send(block(p, i), block(p, i), bsem.at[64 + p], ftr.at[p * 16 + i], dev)

    def send_top(p, i, dev):
        send(top(p, i), top(p, i), bsem.at[64 + p], ftr.at[p * 16 + i], dev)

    def send_bottom(p, i, dev):
        send(bottom(p, i), bottom(p, i), bsem.at[64 + p], fbr.at[p * 16 + i], dev)

    def ready(p, i):
        wait(block(p, i), ftr.at[p * 16 + i])
        return i

    def wait_halves(p, i):
        wait(top(p, i), ftr.at[p * 16 + i])
        wait(bottom(p, i), fbr.at[p * 16 + i])

    def fan(p, i):
        send_block(p, i, peer(a_up, b))
        send_block(p, i, peer(a_down, b))

    def pass_b(p):
        i = ready(p, blk(a, b_down))
        send_top(p, i, peer(a, b_up))
        fan(p, i)
        i = ready(p, blk(a, b_up))
        send_bottom(p, i, peer(a, b_down))
        fan(p, i)
        i = blk(a, b_far)
        wait_halves(p, i)
        fan(p, i)

    def order(b_, n):
        step = jnp.where(n == 0, 0, jnp.where(n == 1, 3, n - 1))
        return lax.rem(b_ + step, 4)

    def near(p):
        def step(n):
            bn = order(b, n)
            i = ready(p, blk(a_down, bn))
            send_top(p, i, peer(a_up, b))
            k = ready(p, blk(a_up, bn))
            send_bottom(p, k, peer(a_down, b))
            if p == 2:
                each(8 * n + 1, 8 * n + 8, send_squares)
            if p % 2 == 1:
                multiply(p // 2, blk(a, bn), i, k)

        each(0, 4, step)

    def far(p):
        def step(n):
            blocks = [blk(a_far, order(b, 2 * n + e)) for e in (0, 1)]
            for i in blocks:
                wait_halves(p, i)
            if p % 2 == 1:
                multiply(p // 2, *blocks)

        each(0, 2, step)
        if p % 2 == 1:
            send(acc.at[1, p // 2], racc.at[p // 2], bsem.at[36 + p // 2], rar.at[p // 2], sib)

    entries = acc.shape[2]
    offset = (j * 8 + z) * entries
    slot = c * 8 + z

    def statistics(pair, sum_sq):
        wait(racc.at[pair], rar.at[pair])
        entry = (offset + lax.broadcasted_iota(jnp.int32, (entries, 128), 0)).astype(F32)
        for g in (0, 1):
            n = pair * 2 + g
            cols = slice(g * 128, (g + 1) * 128)
            logits = (acc[0, pair, :, cols] + racc[pair, :, cols]) * lax.rsqrt(
                sum_sq[n : n + 1] * (1.0 / 8192.0) + epsilon
            )
            peak = jnp.max(logits, axis=0, keepdims=True)
            fs[slot, n : n + 1, :] = peak
            fs[slot, 4 + n : 5 + n, :] = jnp.sum(jnp.exp(logits - peak), axis=0, keepdims=True)
            fs[slot, 8 + n : 9 + n, :] = jnp.sum(
                jnp.where(entry == toks[n : n + 1, :], logits, 0.0), axis=0, keepdims=True
            )

    def start_attention(p):
        gather_sib(p, qkv, 10, g2r, g3r)
        attend(c, p)

    def start_gather(p):
        rotate(p)
        gather_a(p, qkv, 8, g2r)

    def share_heads(p):
        gather_sib(p, ho, 26, h2r, h3r)

    stages = (
        reduce_a,
        reduce_b,
        start_gather,
        start_attention,
        attend_sib,
        join_a,
        join_b,
        join_own,
        share_heads,
        project_out,
        attended,
        features,
        pass_b,
        near,
        far,
    )
    for time in range(len(stages) + 3):
        work = [(time - p, p) for p in range(4) if 0 <= time - p < len(stages)]
        work = [w for w in work if w[0] < 12] + [w for w in work[::-1] if w[0] >= 12]
        for stage, p in work:
            if stage == 13 and p == 0:
                copies[4].wait()
                for n in range(4):
                    wait(wv_sib.at[:, n * 1024 : (n + 1) * 1024], wvr.at[n])
            if stage == 14 and p == 3:
                wait(st.at[0:31], asem.at[2])
                sum_sq = st[0]
                for n in range(1, 32):
                    sum_sq = sum_sq + st[n]
                statistics(0, sum_sq)
            stages[stage](p)
        if time == 0:
            send_weights(0)
            angles()
            copies[1].wait()
            turn_keys(c * 2)
        elif time == 1:
            send_weights(1)
            turn_keys((1 - c) * 2)
            copies[2].wait()
        elif time == 2:
            turn_keys(c * 2 + 1)
        elif time == 3:
            turn_keys((1 - c) * 2 + 1)
        elif time == 5:
            send_weights(2)
        elif time == 6:
            send_weights(3)
            copies[3].wait()
        elif time == 7:
            group_raw()
        elif time == 8:
            group_tokens()
        elif time == 14:
            for k in (8, 16, 24):
                send_squares(k)
            att_ref[...] = dot(place_t[rows(z * 64, 64), :], attz[...]).astype(BF16)
    statistics(1, sum_sq)
    fs[slot, 12:16, :] = jnp.zeros((4, 128), F32)

    def send_stats(k):
        i = lax.rem(slot + k, 16)
        send(fs.at[slot], fs.at[slot], bsem.at[70], asem.at[3], (lax.div(i, 8), s, lax.rem(i, 8)))

    each(1, 16, send_stats)

    def join_stats(ref, count):
        top = ref[0, 0:4, :]
        for n in range(1, count):
            top = jnp.maximum(top, ref[n, 0:4, :])
        exp_total = jnp.zeros((4, 128), F32)
        picked_total = jnp.zeros((4, 128), F32)
        for n in range(count):
            exp_total = exp_total + ref[n, 4:8, :] * jnp.exp(ref[n, 0:4, :] - top)
            picked_total = picked_total + ref[n, 8:12, :]
        return top, exp_total, picked_total

    wait(fs.at[0:15], asem.at[3])
    top, exp_total, picked_total = join_stats(fs, 16)
    fz[s, 0:4, :] = top
    fz[s, 4:8, :] = exp_total
    fz[s, 8:12, :] = picked_total
    fz[s, 12:16, :] = jnp.zeros((4, 128), F32)

    def send_final(k):
        send(fz.at[s], fz.at[s], bsem.at[72], asem.at[4], (c, lax.rem(s + k, 16), z))

    each(1, 16, send_final)
    wait(fz.at[0:15], asem.at[4])
    top, exp_total, picked_total = join_stats(fz, 16)
    grouped = picked_total - top - jnp.log(exp_total)
    cols = []
    for t in range(4):
        first, second = grouped[t % 2 * 2 : t % 2 * 2 + 1], grouped[t % 2 * 2 + 1 : t % 2 * 2 + 2]
        if t // 2 == 0:
            second = pltpu.roll(second, 64, 1)
        else:
            first = pltpu.roll(first, 64, 1)
        cols.append(column(jnp.where(lane[0:1] < 64, first, second)))
    for e in range(4):
        lp_ref[e : e + 1, :] = sum(
            jnp.sum(
                jnp.where(
                    place[t * 128 : (t + 1) * 128, e * 128 : (e + 1) * 128].astype(F32) > 0.0,
                    cols[t],
                    0.0,
                ),
                axis=0,
                keepdims=True,
            )
            for t in range(4)
        )

    wait(xn.at[0:496], bsem.at[0])
    wait(xn.at[0:496], bsem.at[1])
    for p in range(4):
        wait(r1.at[p], bsem.at[4 + p])
        wait(r2.at[p, 0:3], bsem.at[8 + p])
        wait(r3.at[p, 0:3], bsem.at[12 + p])
        wait(qkv.at[0:48], bsem.at[16 + p])
        wait(qkv.at[0:64], bsem.at[20 + p])
        wait(rc1.at[p], bsem.at[24 + p])
        wait(rc2.at[p, 0:3], bsem.at[32 + p])
        wait(rc3.at[p, 0:3], bsem.at[40 + p])
        wait(ho.at[0:48], bsem.at[48 + p])
        wait(ho.at[0:64], bsem.at[52 + p])
        wait(zr.at[p, 0:7], bsem.at[56 + p])
        wait(zr.at[p, 0:7], bsem.at[60 + p])
        wait(feat.at[0, 0:15, :, 0:128], bsem.at[64 + p])
    for pair in (0, 1):
        wait(racc.at[pair], bsem.at[36 + pair])
    wait(st.at[0:31], bsem.at[68])
    wait(wv_sib, bsem.at[28])
    wait(fs.at[0:15], bsem.at[70])
    wait(fz.at[0:15], bsem.at[72])


def per_device(
    x_rows,
    attn_gain,
    final_gain,
    w_query,
    w_kv,
    w_out,
    kv_cache,
    w_vocab,
    token_ids,
    cache_len,
    row_traj,
):
    entries = w_vocab.shape[1]
    spread = np.exp(np.arange(HD // 2) * (-2.0 * math.log(rope_base) / HD)).astype(np.float32)
    vmem = pl.BlockSpec(memory_space=pltpu.VMEM)
    smem = pl.BlockSpec(memory_space=pltpu.SMEM)
    hbm = pl.BlockSpec(memory_space=pl.ANY)
    dma = pltpu.SemaphoreType.DMA
    attended, logprob = pl.pallas_call(
        kernel,
        out_shape=(
            jax.ShapeDtypeStruct((64, 256), BF16),
            jax.ShapeDtypeStruct((4, 128), F32),
        ),
        in_specs=[vmem, vmem, vmem, hbm, vmem, hbm, hbm, hbm, vmem, smem, vmem, vmem],
        out_specs=(vmem, vmem),
        scratch_shapes=[
            pltpu.VMEM((256, 1024), BF16),
            pltpu.VMEM((1024, 256), BF16),
            pltpu.VMEM((4, 1024, 128), BF16),
            pltpu.VMEM((4, 256, 1024), BF16),
            pltpu.VMEM((4, 1024, 256), BF16),
            pltpu.VMEM((entries, 4096), BF16),
            pltpu.VMEM((entries, 4096), BF16),
            pltpu.VMEM((16, 8192), BF16),
            pltpu.VMEM((512, 256), BF16),
            pltpu.VMEM((512, 256), BF16),
            pltpu.VMEM((4, 16, 256), F32),
            pltpu.VMEM((512, 512), BF16),
            pltpu.VMEM((512, 512), BF16),
            pltpu.VMEM((4, 128), F32),
            pltpu.VMEM((4, 2, 16, 128), F32),
            pltpu.VMEM((512, 256), BF16),
            pltpu.VMEM((512, 1280), F32),
            pltpu.VMEM((4, 64, 1280), F32),
            pltpu.VMEM((4, 4, 16, 1280), BF16),
            pltpu.VMEM((4, 4, 16, 1280), BF16),
            pltpu.VMEM((4, 16, 1280), F32),
            pltpu.VMEM((4, 4, 16, 1280), F32),
            pltpu.VMEM((512, 1280), BF16),
            pltpu.VMEM((512, 1152), F32),
            pltpu.VMEM((4, 64, 1152), F32),
            pltpu.VMEM((4, 4, 16, 1152), BF16),
            pltpu.VMEM((4, 4, 16, 1152), BF16),
            pltpu.VMEM((4, 16, 1024), F32),
            pltpu.VMEM((4, 16, 128), F32),
            pltpu.VMEM((4, 4, 16, 1152), BF16),
            pltpu.VMEM((512, 1024), BF16),
            pltpu.VMEM((512, 256), F32),
            pltpu.VMEM((512, 256), BF16),
            pltpu.VMEM((4, 8, 16, 256), BF16),
            pltpu.VMEM((512, 256), BF16),
            pltpu.VMEM((2, 16, 256, 256), BF16),
            pltpu.VMEM((2, 2, entries, 256), F32),
            pltpu.VMEM((2, entries, 256), F32),
            pltpu.VMEM((32, 8, 128), F32),
            pltpu.VMEM((16, 16, 128), F32),
            pltpu.VMEM((16, 16, 128), F32),
            dma((5,)),
            dma((76,)),
            dma((5,)),
            dma((4,)),
            dma((16,)),
            dma((16,)),
            dma((16,)),
            dma((4,)),
            dma((4,)),
            dma((16,)),
            dma((16,)),
            dma((16,)),
            dma((4,)),
            dma((32,)),
            dma((32,)),
            dma((64,)),
            dma((64,)),
            dma((4,)),
            dma((2,)),
        ],
        compiler_params=pltpu.CompilerParams(
            collective_id=0, has_side_effects=True, vmem_limit_bytes=60 * 1024 * 1024
        ),
        cost_estimate=pl.CostEstimate(
            flops=8_000_000_000, bytes_accessed=14_000_000, transcendentals=5_000_000
        ),
    )(
        x_rows,
        attn_gain.reshape(64, 128),
        final_gain.reshape(64, 128),
        w_query,
        w_kv,
        w_out,
        kv_cache,
        w_vocab.T,
        token_ids.reshape(4, 128),
        cache_len,
        row_traj.reshape(4, 128),
        jnp.asarray(np.concatenate([spread, spread])[None]),
    )
    return attended, logprob.reshape(-1)


def solution(mesh):
    in_specs = (
        P(("side", "seq"), None),
        P(),
        P(),
        P(("side", "seq"), "tensor"),
        P(("side", "seq"), None, "tensor"),
        P("tensor", ("side", "seq")),
        P(None, None, ("side", "seq"), "tensor"),
        P(None, ("side", "seq", "tensor")),
        P(),
        P(),
        P(),
    )
    out_specs = (P("tensor", ("side", "seq")), P())
    return jax.shard_map(
        per_device, mesh=mesh, in_specs=in_specs, out_specs=out_specs, check_vma=False
    )
```

time: 740 us -> 127 us (0.17)
  blocking collectives: 414 us -> 0 us
  waiting for transfers between devices: 241 us -> 0 us
  Pallas kernels: 0 us -> 123 us
  matrix products: 27.6 us -> 0 us
  other arithmetic: 23.1 us -> 0 us
  between operations: 14.1 us -> 0.64 us
  local copies, waits for them, and re-layouts: 11.7 us -> 2.62 us
  starting transfers between devices: 7.49 us -> 0 us
    pmax x2 -> x0, blocking collectives: 203 us -> none  [the longest x1 127 us: per_device(): global_peak = lax.pmax(partial_value[0], ('side', 'seq'))]
    psum x2 -> x0, blocking collectives: 198 us -> none  [the longest x1 124 us: per_device(): lax.psum((partial_value[1] * factor, partial_value[2] * factor[..., None]...]
    psum x3 -> x0, waiting for transfers between devices: 171 us -> none  [the longest x1 114 us: per_device(): query_sum, pair_sum = lax.psum((query_part, pair_part), ('side', 'seq'))]
    pallas_call x0 -> x1, Pallas kernels: none -> 123 us  [per_device(): pl.pallas_call(kernel, out_shape=(jax.ShapeDtypeStruct((64, 256), BF16),...]
    all_gather x1 -> x0, waiting for transfers between devices: 62.5 us -> none  [per_device(): lax.all_gather(attended_block, ('side', 'seq'), axis=1, tiled=True)]
    dot_general x10 -> x0, matrix products: 27.6 us -> none  [the longest x2 11.1 us: block_terms(): jnp.einsum('bskgp,bpkd->bskgd', weights.astype(jnp.bfloat16), values_bloc...]
    all_to_all x1 -> x0, blocking collectives: 12.2 us -> none  [per_device(): lax.all_to_all(x_rows, ('side', 'seq'), split_axis=1, concat_axis=0, tile...]
    reduce_sum x6 -> x0, other arithmetic: 11.4 us -> none  [the longest x2 6.38 us: rms_scale(): mean_sq = jnp.mean(values * values, axis=-1, keepdims=True)]
  transfers between devices with their start and end apart: 5 -> 0, of which waited for: 4 -> 0; matrix products, arithmetic and copies ran while one was open for 1% -> 0% of each run, Pallas kernels for 0% -> 0%
where the time goes in v4:
time: 127 us
  Pallas kernels  123 us (97%)
  local copies, waits for them, and re-layouts  2.62 us (2%)
    pallas_call x1, Pallas kernels, per_device(): pl.pallas_call(kernel, out_shape=(jax.ShapeDtypeStruct((64, 256), BF16),...  123 us
    unnamed x2, local copies, waits for them, and re-layouts  2.62 us

profile of v4, /device:TPU:32, one launch (start us, length us, event | category | flops | bytes accessed | tf_op | source)
XLA Modules:
  0.0 126.6 jit_solution(12741450837807928891)
XLA Ops:
  0.6 123.3 %shard_map.131 = (bf16[64,256]{1,0:T(8,128)(2,1)}, f32[4,128]{1,0:T(4,128)}) custom-call(bf16[16,8192]{1,0:T(8,128)(2,1)} %x_ref.1, bf16[64,128]{1,0:T(8,128)(2,1)} %bitcast.8, bf16[64,128]{1,0:T(8,128)(2,1)} %bitcast.9, bf16[256,1024]{1,0:T(8,128)(2,1)} %wq_hbm.1, bf16[256,2,128]{2,1,0:T(2,128)(2,1)} %wkv_ref.1, bf16[1024,256]{1,0:T(8,128)(2,1)} %wo_hbm.1, ...), custom_call_target="tpu_custom_call" | custom-call | flops 8000000000 | bytes 14000000 | tf_op jit(solution)/shard_map/pallas_call | solution.py:822
  123.9 1.4 %copy.16 = bf16[64,256]{1,0:T(8,128)(2,1)} copy(bf16[64,256]{1,0:T(8,128)(2,1)} %get-tuple-element.8) | data formatting | bytes 65536
  125.3 1.2 copy.17
